TPU v7x, 32 devices: a whole 2x2x4 slice. The times are simulated.
32 devices in a mesh: task: 2 (over y), shard: 16 (over z, x, core).
Axes of the slice: x: 2, y: 2, z: 4, core: 2. Of those that a mesh axis runs over, the one named last changes fastest.
Arguments:
- acts: bfloat16 [2, 1024, 4096], P('task', 'shard'), may hold values from -6 to 6
- cotangents: bfloat16 [2, 1024, 16384], P('task', 'shard'), may hold values from -0.75 to 0.75
- task_weights: bfloat16 [2, 4096, 16384], P('task', None, 'shard'), may hold values from -6 to 6
- example_count: int32 [2], P('task'), may hold values from 3 to 8, as said below
- example_start: int32 [2, 8], P('task'), may hold values from 0 to 1023, as said below
- example_len: int32 [2, 8], P('task'), may hold values from 1 to 128, as said below
Outputs:
- merged: bfloat16 [4096, 16384], P('task', 'shard')
Inputs may be any that keep to these rules, and one draw needn't show every extreme that they name: Task t's examples are counted in slots 0 to example_count[t] - 1; some task has 8. Slot e of every task lies in rows e * 128 to (e + 1) * 128 - 1: example_start[t, e] >= e * 128 and example_start[t, e] + example_len[t, e] <= (e + 1) * 128. `example_len`: every task has a counted slot of exactly 128 rows.
All inputs are finite; a program needn't handle non-finite values.
Results may differ from a plain program's by a relative error of at most 0.007.
Values may be sent and summed in bfloat16 or wider, within the bound.
No kernel may reach another device: no remote copies, remote signals or barrier semaphores. Data moves between devices by JAX's collectives and lax.ppermute only.
A program may use at most 128 MiB of HBM per device.

v0:
```python
import jax
import jax.numpy as jnp
from jax import lax
from jax.sharding import PartitionSpec as P

MOST = 128


def per_device(acts, cotangents, task_weights, example_count, example_start, example_len):
    count = example_count[0]
    starts = example_start[0]
    lengths = example_len[0]
    rows = lax.all_gather(acts[0], "shard", axis=0, tiled=True)
    grads = lax.all_to_all(cotangents[0], "shard", split_axis=1, concat_axis=0, tiled=True)
    width = grads.shape[1]

    def one_slot(slot, total):
        block_x = lax.dynamic_slice_in_dim(rows, slot * MOST, MOST, 0)
        block_g = lax.dynamic_slice_in_dim(grads, slot * MOST, MOST, 0)
        position = slot * MOST + jnp.arange(MOST, dtype=jnp.int32)
        first = starts[slot]
        keep = (position >= first) & (position < first + lengths[slot]) & (slot < count)
        masked = jnp.where(keep[:, None], block_g, jnp.zeros_like(block_g))
        grad = lax.dot_general(
            block_x, masked, (((0,), (0,)), ((), ())), preferred_element_type=jnp.float32
        )
        return total + grad * grad

    empty = jnp.zeros((rows.shape[1], width), jnp.float32)
    total = lax.fori_loop(0, starts.shape[0], one_slot, empty)
    fisher = (total / count.astype(jnp.float32)).astype(jnp.bfloat16)
    fisher_parts, weight_parts = (
        lax.all_to_all(fisher[None], "task", split_axis=1, concat_axis=0, tiled=True),
        lax.all_to_all(task_weights, "task", split_axis=1, concat_axis=0, tiled=True),
    )
    weight_f = fisher_parts.astype(jnp.float32)
    numer = jnp.sum(weight_f * weight_parts.astype(jnp.float32), axis=0)
    denom = jnp.sum(weight_f, axis=0) + 1e-06
    return (numer / denom).astype(jnp.bfloat16)


def solution(mesh):
    in_specs = (
        P("task", "shard", None),
        P("task", "shard", None),
        P("task", None, "shard"),
        P("task"),
        P("task", None),
        P("task", None),
    )
    out_specs = P("task", "shard")
    return jax.shard_map(
        per_device, mesh=mesh, in_specs=in_specs, out_specs=out_specs, check_vma=False
    )
```

profile of v0, /device:TPU:0, one launch (start us, length us, event | category | flops | bytes accessed | tf_op | source)
XLA Modules:
  0.0 527.0 jit_solution(14574014394086275979)
XLA Ops:
  12.5 7.4 %all-to-all-start = ((bf16[64,16,1024]{2,0,1:T(8,128)(2,1)}), bf16[64,16,1024]{2,0,1:T(8,128)(2,1)S(1)}, u32[]{:S(2)}, u32[]{:S(2)}) async-start(bf16[64,16,1024]{2,0,1:T(8,128)(2,1)} %copy.10), calls=%async_computation | async-start | bytes 4194304 | tf_op jit(solution)/shard_map/all_to_all | solution.py:14
  20.6 15.5 %copy.18 = bf16[1,4096,1024]{2,0,1:T(2,128)(2,1)} copy(bf16[1,4096,1024]{2,1,0:T(8,128)(2,1)} %param.10) | data formatting | bytes 16777216 | tf_op args[2]
  36.5 49.4 %reduce.1 = bf16[4096,1024]{1,0:T(8,128)(2,1)} reduce(bf16[4096,1,1024]{2,1,0:T(2,128)(2,1)} %bitcast.32, bf16[]{:T(256)} %broadcast.42), dimensions={1}, to_apply=%bitcast.23.reduce_sub_computation | reduce | bytes 16777218
  86.0 10.2 %reshape.27 = bf16[2,2,1048576]{2,1,0:T(2,128)(2,1)} reshape(bf16[4096,1024]{1,0:T(8,128)(2,1)} %reduce.1) | data formatting | bytes 16777216
  103.4 18.7 %all-gather.3.cloned.1.call-done = bf16[1,1024,4096]{2,1,0:T(8,128)(2,1)} async-done(((bf16[1,64,4096]{2,1,0:T(8,128)(2,1)}), bf16[1,1024,4096]{2,1,0:T(8,128)(2,1)}) %all-gather.3.cloned.1.call-update) | async-done | bytes 8388624 | tf_op jit(solution)/shard_map/all_gather | solution.py:13
  122.1 116.6 %while.14 = (s32[]{:T(128)}, f32[4096,1024]{1,0:T(8,128)}, bf16[1024,4096]{1,0:T(8,128)(2,1)}, s32[8]{0:T(128)S(1)}, s32[8]{0:T(128)S(1)}, /*index=5*/s32[]{:T(1...) while((s32[]{:T(128)}, f32[4096,1024]{1,0:T(8,128)}, ...), condition=%wide.region_1.2_spmd.clone, body=%wide.region_0.1_spmd.clone.sunk | while | flops 1086456448 | bytes 34867556 | solution.py:30
  126.0 8.4 %select_add_fusion.2 = f32[4096,1024]{1,0:T(8,128)} fusion(f32[4096,1024]{1,0:T(8,128)} %get-tuple-element.225, pred[]{:T(512)S(6)} %compare.3, bf16[1024,4096]{1,0:T(8,128)(2,1)} %get-tuple-element.237, s32[]{:T(128)S(6)} %select_n.29, bf16[1024,1024]{1,0:T(8,128)(2,1)S(1)} %get-tuple-element.241, pred[128]{0:T(512)(128)(4,1)S(1)} %and_and_fusion.2), kind=kOutput, calls=%fused_computation.clone.1 | convolution fusion | flops 1086455808 | bytes 34867200 | tf_op jit(solution)/shard_map/while/body/eval_jaxpr/dot_general | solution.py:24
  138.3 11.0 %select_add_fusion.2 = f32[4096,1024]{1,0:T(8,128)} fusion(f32[4096,1024]{1,0:T(8,128)} %get-tuple-element.225, pred[]{:T(512)S(6)} %compare.3, bf16[1024,4096]{1,0:T(8,128)(2,1)} %get-tuple-element.237, s32[]{:T(128)S(6)} %select_n.29, bf16[1024,1024]{1,0:T(8,128)(2,1)S(1)} %get-tuple-element.241, pred[128]{0:T(512)(128)(4,1)S(1)} %and_and_fusion.2), kind=kOutput, calls=%fused_computation.clone.1 | convolution fusion | flops 1086455808 | bytes 34867200 | tf_op jit(solution)/shard_map/while/body/eval_jaxpr/dot_general | solution.py:24
  153.2 11.0 %select_add_fusion.2 = f32[4096,1024]{1,0:T(8,128)} fusion(f32[4096,1024]{1,0:T(8,128)} %get-tuple-element.225, pred[]{:T(512)S(6)} %compare.3, bf16[1024,4096]{1,0:T(8,128)(2,1)} %get-tuple-element.237, s32[]{:T(128)S(6)} %select_n.29, bf16[1024,1024]{1,0:T(8,128)(2,1)S(1)} %get-tuple-element.241, pred[128]{0:T(512)(128)(4,1)S(1)} %and_and_fusion.2), kind=kOutput, calls=%fused_computation.clone.1 | convolution fusion | flops 1086455808 | bytes 34867200 | tf_op jit(solution)/shard_map/while/body/eval_jaxpr/dot_general | solution.py:24
  168.1 11.0 %select_add_fusion.2 = f32[4096,1024]{1,0:T(8,128)} fusion(f32[4096,1024]{1,0:T(8,128)} %get-tuple-element.225, pred[]{:T(512)S(6)} %compare.3, bf16[1024,4096]{1,0:T(8,128)(2,1)} %get-tuple-element.237, s32[]{:T(128)S(6)} %select_n.29, bf16[1024,1024]{1,0:T(8,128)(2,1)S(1)} %get-tuple-element.241, pred[128]{0:T(512)(128)(4,1)S(1)} %and_and_fusion.2), kind=kOutput, calls=%fused_computation.clone.1 | convolution fusion | flops 1086455808 | bytes 34867200 | tf_op jit(solution)/shard_map/while/body/eval_jaxpr/dot_general | solution.py:24
  183.0 11.0 %select_add_fusion.2 = f32[4096,1024]{1,0:T(8,128)} fusion(f32[4096,1024]{1,0:T(8,128)} %get-tuple-element.225, pred[]{:T(512)S(6)} %compare.3, bf16[1024,4096]{1,0:T(8,128)(2,1)} %get-tuple-element.237, s32[]{:T(128)S(6)} %select_n.29, bf16[1024,1024]{1,0:T(8,128)(2,1)S(1)} %get-tuple-element.241, pred[128]{0:T(512)(128)(4,1)S(1)} %and_and_fusion.2), kind=kOutput, calls=%fused_computation.clone.1 | convolution fusion | flops 1086455808 | bytes 34867200 | tf_op jit(solution)/shard_map/while/body/eval_jaxpr/dot_general | solution.py:24
  197.9 11.0 %select_add_fusion.2 = f32[4096,1024]{1,0:T(8,128)} fusion(f32[4096,1024]{1,0:T(8,128)} %get-tuple-element.225, pred[]{:T(512)S(6)} %compare.3, bf16[1024,4096]{1,0:T(8,128)(2,1)} %get-tuple-element.237, s32[]{:T(128)S(6)} %select_n.29, bf16[1024,1024]{1,0:T(8,128)(2,1)S(1)} %get-tuple-element.241, pred[128]{0:T(512)(128)(4,1)S(1)} %and_and_fusion.2), kind=kOutput, calls=%fused_computation.clone.1 | convolution fusion | flops 1086455808 | bytes 34867200 | tf_op jit(solution)/shard_map/while/body/eval_jaxpr/dot_general | solution.py:24
  212.8 11.0 %select_add_fusion.2 = f32[4096,1024]{1,0:T(8,128)} fusion(f32[4096,1024]{1,0:T(8,128)} %get-tuple-element.225, pred[]{:T(512)S(6)} %compare.3, bf16[1024,4096]{1,0:T(8,128)(2,1)} %get-tuple-element.237, s32[]{:T(128)S(6)} %select_n.29, bf16[1024,1024]{1,0:T(8,128)(2,1)S(1)} %get-tuple-element.241, pred[128]{0:T(512)(128)(4,1)S(1)} %and_and_fusion.2), kind=kOutput, calls=%fused_computation.clone.1 | convolution fusion | flops 1086455808 | bytes 34867200 | tf_op jit(solution)/shard_map/while/body/eval_jaxpr/dot_general | solution.py:24
  227.7 11.0 %select_add_fusion.2 = f32[4096,1024]{1,0:T(8,128)} fusion(f32[4096,1024]{1,0:T(8,128)} %get-tuple-element.225, pred[]{:T(512)S(6)} %compare.3, bf16[1024,4096]{1,0:T(8,128)(2,1)} %get-tuple-element.237, s32[]{:T(128)S(6)} %select_n.29, bf16[1024,1024]{1,0:T(8,128)(2,1)S(1)} %get-tuple-element.241, pred[128]{0:T(512)(128)(4,1)S(1)} %and_and_fusion.2), kind=kOutput, calls=%fused_computation.clone.1 | convolution fusion | flops 1086455808 | bytes 34867200 | tf_op jit(solution)/shard_map/while/body/eval_jaxpr/dot_general | solution.py:24
  245.8 56.5 %copy.19 = bf16[1,4096,1024]{2,0,1:T(2,128)(2,1)} copy(bf16[1,4096,1024]{2,1,0:T(8,128)(2,1)S(1)} %fusion.8) | data formatting | bytes 16777216 | tf_op jit(solution)/shard_map/broadcast_in_dim | solution.py:33
  302.3 49.4 %reduce = bf16[4096,1024]{1,0:T(8,128)(2,1)} reduce(bf16[4096,1,1024]{2,1,0:T(2,128)(2,1)} %bitcast.33, bf16[]{:T(256)} %broadcast.42), dimensions={1}, to_apply=%bitcast.24.reduce_sub_computation | reduce | bytes 16777218
  351.8 10.2 %reshape.25 = bf16[2,2,1048576]{2,1,0:T(2,128)(2,1)} reshape(bf16[4096,1024]{1,0:T(8,128)(2,1)} %reduce) | data formatting | bytes 16777216
  369.1 17.8 %reshape.28 = bf16[4096,1,1024]{2,1,0:T(2,128)(2,1)} reshape(bf16[2,2,1048576]{2,1,0:T(2,128)(2,1)} %all-to-all-done.2) | data formatting | bytes 16777216
  386.9 12.1 %copy.13 = bf16[1,4096,1024]{2,1,0:T(8,128)(2,1)} copy(bf16[1,4096,1024]{2,0,1:T(2,128)(2,1)} %bitcast.30) | data formatting | bytes 16777216 | tf_op jit(solution)/shard_map/all_to_all | solution.py:34
  399.0 63.1 %all-to-all-done.1 = bf16[2,2,1048576]{2,1,0:T(2,128)(2,1)} async-done(((bf16[2,2,1048576]{2,1,0:T(2,128)(2,1)}), bf16[2,2,1048576]{2,1,0:T(2,128)(2,1)}, u32[]{:S(2)}, u32[]{:S(2)}) %all-to-all-start.1) | async-done | bytes 8388640 | tf_op jit(solution)/shard_map/all_to_all | solution.py:33
  462.1 17.8 %reshape.26 = bf16[4096,1,1024]{2,1,0:T(2,128)(2,1)} reshape(bf16[2,2,1048576]{2,1,0:T(2,128)(2,1)} %all-to-all-done.1) | data formatting | bytes 16777216
  479.9 14.9 %copy.14 = f32[1,4096,1024]{2,1,0:T(8,128)} copy(bf16[1,4096,1024]{2,0,1:T(2,128)(2,1)} %bitcast.34) | data formatting | bytes 25165824
  494.8 14.9 %fusion.9 = (f32[2048,1024]{1,0:T(8,128)}, f32[2048,1024]{1,0:T(8,128)}) fusion(f32[2,2048,1024]{2,1,0:T(8,128)} %bitcast.31, bf16[2,2048,1024]{2,1,0:T(8,128)(2,1)S(1)} %bitcast.35), kind=kLoop, calls=%fused_computation.14 | loop fusion | flops 12582912 | bytes 41943040 | tf_op jit(solution)/shard_map/reduce_sum | solution.py:38
  509.7 10.0 %divide_convert_fusion.1 = bf16[2048,1024]{1,0:T(8,128)(2,1)} fusion(f32[2048,1024]{1,0:T(8,128)} %get-tuple-element.155, f32[2048,1024]{1,0:T(8,128)} %get-tuple-element.154), kind=kLoop, calls=%fused_computation.12 | loop fusion | flops 6291456 | bytes 20971520 | tf_op jit(solution)/shard_map/convert_element_type | solution.py:39
  (41 shorter events, 43.2 us)
Async XLA Ops:
  6.5 115.6 %all-gather.3.cloned.1.call-start = ((), (), s32[]{:S(2)}) async-start(), calls=%async_computation.3 | async-start | bytes 8912896 | tf_op jit(solution)/shard_map/all_gather | solution.py:13
  12.5 83.7 %all-to-all-start = ((bf16[64,16,1024]{2,0,1:T(8,128)(2,1)}), bf16[64,16,1024]{2,0,1:T(8,128)(2,1)S(1)}, u32[]{:S(2)}, u32[]{:S(2)}) async-start(bf16[64,16,1024]{2,0,1:T(8,128)(2,1)} %copy.10), calls=%async_computation | async-start | bytes 4194304 | tf_op jit(solution)/shard_map/all_to_all | solution.py:14
  96.2 26.0 %copy-start.1 = (s32[1,8]{1,0:T(1,128)S(1)}, s32[1,8]{1,0:T(1,128)}, u32[]{:S(2)}) copy-start(s32[1,8]{1,0:T(1,128)} %param.12) | copy-start | bytes 100
  96.2 26.0 %copy-start.2 = (s32[1,8]{1,0:T(1,128)S(1)}, s32[1,8]{1,0:T(1,128)}, u32[]{:S(2)}) copy-start(s32[1,8]{1,0:T(1,128)} %param.13) | copy-start | bytes 100
  96.2 265.7 %all-to-all-start.2 = ((bf16[2,2,1048576]{2,1,0:T(2,128)(2,1)}), bf16[2,2,1048576]{2,1,0:T(2,128)(2,1)}, u32[]{:S(2)}, u32[]{:S(2)}) async-start(bf16[2,2,1048576]{2,1,0:T(2,128)(2,1)} %reshape.27), calls=%async_computation.2 | async-start | bytes 16777216 | tf_op jit(solution)/shard_map/all_to_all | solution.py:34
  361.9 100.2 %all-to-all-start.1 = ((bf16[2,2,1048576]{2,1,0:T(2,128)(2,1)}), bf16[2,2,1048576]{2,1,0:T(2,128)(2,1)}, u32[]{:S(2)}, u32[]{:S(2)}) async-start(bf16[2,2,1048576]{2,1,0:T(2,128)(2,1)} %reshape.25), calls=%async_computation.1 | async-start | bytes 16777216 | tf_op jit(solution)/shard_map/all_to_all | solution.py:33
  479.9 14.9 %copy-start = (bf16[1,4096,1024]{2,1,0:T(8,128)(2,1)S(1)}, bf16[1,4096,1024]{2,1,0:T(8,128)(2,1)}, u32[]{:S(2)}) copy-start(bf16[1,4096,1024]{2,1,0:T(8,128)(2,1)} %copy.13) | copy-start | bytes 25165828
Sparse Core Ops, SparseCore 0:
  9.5 112.5 all-gather.2
where the time goes:
time: 535 us; the launch traced here: 527 us
  local copies, waits for them, and re-layouts  171 us (32%)
  other arithmetic  136 us (25%)
  matrix products  85.4 us (16%)
  waiting for transfers between devices  82.5 us (15%)
  starting transfers between devices  21.8 us (4%)
  loops' own time  16 us (3%)
  between operations  14.6 us (3%)
    unnamed x3, other arithmetic  98.9 us
    unnamed x14, local copies, waits for them, and re-layouts  89.6 us
    dot_general x8, matrix products, one_slot(): lax.dot_general(block_x, masked, (((0,), (0,)), ((), ())), preferred_elem...  85.4 us
    all_to_all x1, waiting for transfers between devices, per_device(): lax.all_to_all(fisher[None], 'task', split_axis=1, concat_axis=0, tiled=T...  63.1 us
    broadcast_in_dim x1, local copies, waits for them, and re-layouts, per_device(): fisher[None]  56.5 us
    all_gather x1, waiting for transfers between devices, per_device(): rows = lax.all_gather(acts[0], 'shard', axis=0, tiled=True)  18.7 us
    another operation x1, loops' own time, per_device(): total = lax.fori_loop(0, starts.shape[0], one_slot, empty)  16 us
    reduce_sum x1, other arithmetic, per_device(): denom = jnp.sum(weight_f, axis=0) + 1e-06  14.9 us
  transfers between devices with their start and end apart: 4, of which 2 were waited for; matrix products, arithmetic and copies ran while one was open for 63% of the time, Pallas kernels for 0%

commit v1 on v0

v1 whole, which is shorter than its diff:
```python
import functools

import jax
import jax.numpy as jnp
from jax import lax
from jax.experimental import pallas as pl
from jax.experimental.pallas import tpu as pltpu
from jax.sharding import PartitionSpec as P


def tile(size, most):
    part = size
    while part > most and part % 2 == 0:
        part //= 2
    return part


def fisher_rows(table_ref, task, x_ref, g_ref, slots, columns):
    devices, _, rows_each, width = x_ref.shape
    per_slot = rows_each * devices // slots
    spread = devices // slots
    total = None
    for slot in range(slots):
        x = x_ref[slot * spread : (slot + 1) * spread, 0].reshape(per_slot, width)
        row = slot * per_slot + lax.broadcasted_iota(jnp.int32, (per_slot, width), 0)
        first = table_ref[task, 1 + slot]
        last = first + table_ref[task, 1 + slots + slot]
        keep = (row >= first) & (row < last) & (slot < table_ref[task, 0])
        x = x * keep.astype(jnp.float32).astype(x.dtype)
        g = g_ref[slot * per_slot : (slot + 1) * per_slot, columns]
        grad = lax.dot_general(x, g, (((0,), (0,)), ((), ())), preferred_element_type=jnp.float32)
        total = grad * grad if total is None else total + grad * grad
    return (total / table_ref[task, 0].astype(jnp.float32)).astype(jnp.bfloat16)


def merge_kernel(tasks, slots, part, table_ref, *refs):
    x_refs, g_refs = refs[:tasks], refs[tasks : 2 * tasks]
    w_refs, out_ref = refs[2 * tasks : 3 * tasks], refs[3 * tasks]
    for start in range(0, out_ref.shape[1], part):
        columns = slice(start, start + part)
        numer, denom = None, None
        for task in range(tasks):
            fisher = fisher_rows(table_ref, task, x_refs[task], g_refs[task], slots, columns)
            fisher = fisher.astype(jnp.float32)
            term = fisher * w_refs[task][:, columns].astype(jnp.float32)
            numer = term if numer is None else numer + term
            denom = fisher if denom is None else denom + fisher
        out_ref[:, columns] = (numer / (denom + 1e-6)).astype(out_ref.dtype)


def per_device(tasks, acts, cotangents, task_weights, example_count, example_start, example_len):
    slots = example_start.shape[1]
    mine = lax.axis_index("task")
    high = acts.shape[2] // tasks
    width = task_weights.shape[2]
    tokens_each = acts.shape[1]

    def hand_on(step, value):
        return lax.ppermute(value, "task", [(i, (i + step) % tasks) for i in range(tasks)])

    def target(step):
        return lax.rem(mine + step, tasks)

    own = jnp.concatenate([example_count, example_start[0], example_len[0]])
    table = jnp.stack([own] + [hand_on(step, own) for step in range(1, tasks)])

    x_parts = []
    for step in range(tasks):
        part = lax.dynamic_slice_in_dim(acts[0], target(step) * high, high, 1)
        x_parts.append(part if step == 0 else hand_on(step, part))
    x = lax.all_gather(jnp.stack(x_parts), "shard", axis=0)

    grads = lax.all_to_all(cotangents[0], "shard", split_axis=1, concat_axis=0, tiled=True)
    g = [grads] + [hand_on(step, grads) for step in range(1, tasks)]

    w = []
    for step in range(tasks):
        part = lax.dynamic_slice_in_dim(task_weights[0], target(step) * high, high, 0)
        w.append(part if step == 0 else hand_on(step, part))

    block = tile(high, 256)
    devices = x.shape[0]
    x_specs = [
        pl.BlockSpec((devices, 1, tokens_each, block), functools.partial(lambda t, i, s: (0, t, 0, i), t))
        for t in range(tasks)
    ]
    g_specs = [pl.BlockSpec(grads.shape, lambda i, s: (0, 0)) for _ in range(tasks)]
    w_spec = pl.BlockSpec((block, width), lambda i, s: (i, 0))
    return pl.pallas_call(
        functools.partial(merge_kernel, tasks, slots, tile(width, 256)),
        out_shape=jax.ShapeDtypeStruct((high, width), jnp.bfloat16),
        grid_spec=pltpu.PrefetchScalarGridSpec(
            num_scalar_prefetch=1,
            grid=(high // block,),
            in_specs=x_specs + g_specs + [w_spec] * tasks,
            out_specs=w_spec,
        ),
        compiler_params=pltpu.CompilerParams(vmem_limit_bytes=48 * 1024 * 1024),
    )(table, *([x] * tasks), *g, *w)


def solution(mesh):
    in_specs = (
        P("task", "shard", None),
        P("task", "shard", None),
        P("task", None, "shard"),
        P("task"),
        P("task", None),
        P("task", None),
    )
    return jax.shard_map(
        functools.partial(per_device, mesh.shape["task"]),
        mesh=mesh,
        in_specs=in_specs,
        out_specs=P("task", "shard"),
        check_vma=False,
    )
```

time: 535 us -> 217 us (0.41); the launches traced: 527 us -> 217 us
  local copies, waits for them, and re-layouts: 171 us -> 17.1 us
  other arithmetic: 136 us -> 1.01 us
  matrix products: 85.4 us -> 0 us
  waiting for transfers between devices: 82.5 us -> 140 us
  Pallas kernels: 0 us -> 31.7 us
  loops' own time: 16 us -> 0 us
  starting transfers between devices: 21.8 us -> 12.7 us
    unnamed x3 -> x0, other arithmetic: 98.9 us -> none
    ppermute x0 -> x4, waiting for transfers between devices: none -> 92.7 us  [hand_on(): lax.ppermute(value, 'task', [(i, (i + step) % tasks) for i in range(tasks)])]
    dot_general x8 -> x0, matrix products: 85.4 us -> none  [one_slot(): lax.dot_general(block_x, masked, (((0,), (0,)), ((), ())), preferred_elem...]
    unnamed x14 -> x9, local copies, waits for them, and re-layouts: 89.6 us -> 5.72 us
    all_to_all x2 -> x0, waiting for transfers between devices: 63.1 us -> none  [the longest x1 63.1 us: per_device(): lax.all_to_all(fisher[None], 'task', split_axis=1, concat_axis=0, tiled=T...]
    broadcast_in_dim x1 -> x0, local copies, waits for them, and re-layouts: 56.5 us -> none  [per_device(): fisher[None]]
    all_to_all x1, waiting for transfers between devices: 0.01 us -> 47.4 us  [per_device(): lax.all_to_all(cotangents[0], 'shard', split_axis=1, concat_axis=0, tiled...]
    pallas_call x0 -> x1, Pallas kernels: none -> 31.7 us  [per_device(): pl.pallas_call(functools.partial(merge_kernel, tasks, slots, tile(width,...]
  transfers between devices with their start and end apart: 4 -> 6, of which waited for: 2 -> 3; matrix products, arithmetic and copies ran while one was open for 63% -> 6% of each run, Pallas kernels for 0% -> 0%
where the time goes in v1:
time: 217 us
  waiting for transfers between devices  140 us (65%)
  Pallas kernels  31.7 us (15%)
  local copies, waits for them, and re-layouts  17.1 us (8%)
  between operations  14.1 us (6%)
  starting transfers between devices  12.7 us (6%)
    ppermute x4, waiting for transfers between devices, hand_on(): lax.ppermute(value, 'task', [(i, (i + step) % tasks) for i in range(tasks)])  92.7 us
    all_to_all x1, waiting for transfers between devices, per_device(): lax.all_to_all(cotangents[0], 'shard', split_axis=1, concat_axis=0, tiled...  47.4 us
    pallas_call x1, Pallas kernels, per_device(): pl.pallas_call(functools.partial(merge_kernel, tasks, slots, tile(width,...  31.7 us
    dynamic_slice x1, local copies, waits for them, and re-layouts, per_device(): lax.dynamic_slice_in_dim(task_weights[0], target(step) * high, high, 0)  7.8 us
    ppermute x4, starting transfers between devices, hand_on(): lax.ppermute(value, 'task', [(i, (i + step) % tasks) for i in range(tasks)])  6.58 us
    all_to_all x1, starting transfers between devices, per_device(): lax.all_to_all(cotangents[0], 'shard', split_axis=1, concat_axis=0, tiled...  6.13 us
    unnamed x9, local copies, waits for them, and re-layouts  5.72 us
  transfers between devices with their start and end apart: 6, of which 3 were waited for; matrix products, arithmetic and copies ran while one was open for 6% of the time, Pallas kernels for 0%

profile of v1, /device:TPU:0, one launch (start us, length us, event | category | flops | bytes accessed | tf_op | source)
XLA Modules:
  0.0 216.6 jit_solution(17866659067200255308)
XLA Ops:
  6.5 1.1 constant_dynamic-slice_fusion
  7.6 3.0 %collective-permute-start.1 = (bf16[64,2048]{1,0:T(8,128)(2,1)S(1)}, bf16[64,2048]{1,0:T(8,128)(2,1)S(1)}, u32[]{:S(2)}, u32[]{:S(2)}) collective-permute-start(bf16[64,2048]{1,0:T(8,128)(2,1)S(1)} %get-tuple-element.8), channel_id=1, source_target_pairs={{0,16},{16,0},{1,17},{17,1},{2,18},{18,2},{3,19},{19,3},{4,20},{20... | collective-permute-start | bytes 786440 | tf_op jit(solution)/shard_map/ppermute | solution.py:59
  10.6 6.3 %collective-permute-done.1 = bf16[64,2048]{1,0:T(8,128)(2,1)S(1)} collective-permute-done((bf16[64,2048]{1,0:T(8,128)(2,1)S(1)}, bf16[64,2048]{1,0:T(8,128)(2,1)S(1)}, u32[]{:S(2)}, u32[]{:S(2)}) %collective-permute-start.1) | collective-permute-done | bytes 262176 | tf_op jit(solution)/shard_map/ppermute | solution.py:59
  16.9 0.8 pad_maximum_fusion
  17.8 0.0 all-gather.3.cloned.1.call-update
  17.8 2.8 %copy.9 = bf16[8,8,16,1024]{3,2,1,0:T(8,128)(2,1)S(1)} copy(bf16[8,8,16,1024]{3,1,2,0:T(8,128)(2,1)} %bitcast.24) | data formatting | bytes 4194304
  20.6 2.5 %copy.8 = bf16[64,16,1024]{2,0,1:T(8,128)(2,1)} copy(bf16[64,16,1024]{2,1,0:T(8,128)(2,1)S(1)} %bitcast.23) | data formatting | bytes 4194304 | tf_op jit(solution)/shard_map/all_to_all | solution.py:73
  23.1 6.1 %all-to-all-start = ((bf16[64,16,1024]{2,0,1:T(8,128)(2,1)}), bf16[64,16,1024]{2,0,1:T(8,128)(2,1)S(1)}, u32[]{:S(2)}, u32[]{:S(2)}) async-start(bf16[64,16,1024]{2,0,1:T(8,128)(2,1)} %copy.8), calls=%async_computation | async-start | bytes 4194304 | tf_op jit(solution)/shard_map/all_to_all | solution.py:73
  29.2 0.0 copy-start.2
  29.3 0.0 copy-start.3
  29.3 7.8 %dynamic-slice_bitcast_fusion = (bf16[2048,1024]{1,0:T(8,128)(2,1)}, bf16[2048,1024]{1,0:T(8,128)(2,1)}) fusion(bf16[1,4096,1024]{2,1,0:T(8,128)(2,1)} %param.8, s32[]{:T(128)S(6)} %select_n.9, s32[]{:T(128)S(6)} %select_n.8), kind=kLoop, calls=%fused_computation | loop fusion | bytes 16777224 | tf_op jit(solution)/shard_map/dynamic_slice | solution.py:78
  37.1 1.5 collective-permute-start.3
  38.6 47.4 %all-to-all-done = bf16[64,16,1024]{2,0,1:T(8,128)(2,1)S(1)} async-done(((bf16[64,16,1024]{2,0,1:T(8,128)(2,1)}), bf16[64,16,1024]{2,0,1:T(8,128)(2,1)S(1)}, u32[]{:S(2)}, u32[]{:S(2)}) %all-to-all-start) | async-done | bytes 2097184 | tf_op jit(solution)/shard_map/all_to_all | solution.py:73
  86.0 1.5 collective-permute-start.2
  88.1 0.1 pad_add_fusion.1
  88.2 0.5 collective-permute-start
  88.8 0.1 fusion
  88.8 86.4 %collective-permute-done = s32[17]{0:T(128)S(1)} collective-permute-done((s32[17]{0:T(128)S(1)}, s32[17]{0:T(128)S(1)}, u32[]{:S(2)}, u32[]{:S(2)}) %collective-permute-start) | collective-permute-done | bytes 100 | tf_op jit(solution)/shard_map/ppermute | solution.py:59
  175.2 0.0 collective-permute-done.3.refs_5_
  175.2 0.0 collective-permute-done.2.refs_3_
  175.2 0.0 copy-start
  175.2 1.3 copy-done
  176.5 1.6 copy-done.1
  178.1 31.7 %shard_map.64 = bf16[2048,1024]{1,0:T(8,128)(2,1)} custom-call(s32[2,17]{1,0:T(2,128)S(1)} %pad_add_fusion.table_ref, bf16[16,2,64,2048]{3,2,1,0:T(8,128)(2,1)} %bitcast.21, bf16[16,2,64,2048]{3,2,1,0:T(8,128)(2,1)} %bitcast.22, bf16[1024,1024]{1,0:T(8,128)(2,1)S(1)} %bitcast.20, bf16[1024,1024]{1,0:T(8,128)(2,1)S(1)} %copy-done.1, ...), custom_call_target="tpu_custom_call" | custom-call | tf_op jit(solution)/shard_map/pallas_call | solution.py:89
  (6 shorter events, 0.0 us)
Async XLA Ops:
  6.5 170.0 %all-gather.3.cloned.1.call-start = ((), (), s32[]{:S(2)}) async-start(), calls=%async_computation.1 | async-start | bytes 8912896 | tf_op jit(solution)/shard_map/all_gather | solution.py:71
  7.6 9.3 %collective-permute-start.1 = (bf16[64,2048]{1,0:T(8,128)(2,1)S(1)}, bf16[64,2048]{1,0:T(8,128)(2,1)S(1)}, u32[]{:S(2)}, u32[]{:S(2)}) collective-permute-start(bf16[64,2048]{1,0:T(8,128)(2,1)S(1)} %get-tuple-element.8), channel_id=1, source_target_pairs={{0,16},{16,0},{1,17},{17,1},{2,18},{18,2},{3,19},{19,3},{4,20},{20... | collective-permute-start | bytes 786440 | tf_op jit(solution)/shard_map/ppermute | solution.py:59
  23.1 62.9 %all-to-all-start = ((bf16[64,16,1024]{2,0,1:T(8,128)(2,1)}), bf16[64,16,1024]{2,0,1:T(8,128)(2,1)S(1)}, u32[]{:S(2)}, u32[]{:S(2)}) async-start(bf16[64,16,1024]{2,0,1:T(8,128)(2,1)} %copy.8), calls=%async_computation | async-start | bytes 4194304 | tf_op jit(solution)/shard_map/all_to_all | solution.py:73
  29.2 58.9 %copy-start.2 = (s32[1,8]{1,0:T(1,128)S(1)}, s32[1,8]{1,0:T(1,128)}, u32[]{:S(2)}) copy-start(s32[1,8]{1,0:T(1,128)} %param.11) | copy-start | bytes 100
  29.3 58.9 %copy-start.3 = (s32[1,8]{1,0:T(1,128)S(1)}, s32[1,8]{1,0:T(1,128)}, u32[]{:S(2)}) copy-start(s32[1,8]{1,0:T(1,128)} %param.10) | copy-start | bytes 100
  37.1 138.1 %collective-permute-start.3 = (bf16[2048,1024]{1,0:T(8,128)(2,1)}, bf16[2048,1024]{1,0:T(8,128)(2,1)}, u32[]{:S(2)}, u32[]{:S(2)}) collective-permute-start(bf16[2048,1024]{1,0:T(8,128)(2,1)} %get-tuple-element.5), channel_id=1, source_target_pairs={{0,16},{16,0},{1,17},{17,1},{2,18},{18,2},{3,19},{19,3},{4,20},{20... | collective-permute-start | bytes 12582920 | tf_op jit(solution)/shard_map/ppermute | solution.py:59
  86.0 89.2 %collective-permute-start.2 = (bf16[1024,1024]{1,0:T(8,128)(2,1)S(1)}, bf16[1024,1024]{1,0:T(8,128)(2,1)S(1)}, u32[]{:S(2)}, u32[]{:S(2)}) collective-permute-start(bf16[1024,1024]{1,0:T(8,128)(2,1)S(1)} %bitcast.19), channel_id=1, source_target_pairs={{0,16},{16,0},{1,17},{17,1},{2,18},{18,2},{3,19},{19,3},{4,20},{20... | collective-permute-start | bytes 6291464 | tf_op jit(solution)/shard_map/ppermute | solution.py:59
  88.2 87.0 %collective-permute-start = (s32[17]{0:T(128)S(1)}, s32[17]{0:T(128)S(1)}, u32[]{:S(2)}, u32[]{:S(2)}) collective-permute-start(s32[17]{0:T(128)S(1)} %pad_add_fusion.1), channel_id=1, source_target_pairs={{0,16},{16,0},{1,17},{17,1},{2,18},{18,2},{3,19},{19,3},{4,20},{20... | collective-permute-start | bytes 212 | tf_op jit(solution)/shard_map/ppermute | solution.py:59
  175.2 1.3 copy-start
  176.5 1.6 copy-start.1
Sparse Core Ops, SparseCore 0:
  17.9 111.1 all-gather.2

commit v2 on v1

v2 whole, which is shorter than its diff:
```python
import functools

import jax
import jax.numpy as jnp
from jax import lax
from jax.experimental import pallas as pl
from jax.experimental.pallas import tpu as pltpu
from jax.sharding import PartitionSpec as P


def tile(size, most):
    part = size
    while part > most and part % 2 == 0:
        part //= 2
    return part


def fisher_rows(table_ref, task, x_ref, g_ref, slots, columns):
    devices, _, rows_each, width = x_ref.shape
    per_slot = rows_each * devices // slots
    spread = devices // slots
    total = None
    for slot in range(slots):
        x = x_ref[slot * spread : (slot + 1) * spread, 0].reshape(per_slot, width)
        g = g_ref[slot * per_slot : (slot + 1) * per_slot, columns]
        grad = lax.dot_general(x, g, (((0,), (0,)), ((), ())), preferred_element_type=jnp.float32)
        total = grad * grad if total is None else total + grad * grad
    return (total / table_ref[task, 0].astype(jnp.float32)).astype(jnp.bfloat16)


def fisher_kernel(task, slots, part, table_ref, x_ref, g_ref, out_ref):
    for start in range(0, out_ref.shape[1], part):
        columns = slice(start, start + part)
        out_ref[:, columns] = fisher_rows(table_ref, task, x_ref, g_ref, slots, columns)


def fisher_of(task, slots, table, x, g, high):
    devices, _, tokens_each, _ = x.shape
    width = g.shape[1]
    block = tile(high, 512)
    return pl.pallas_call(
        functools.partial(fisher_kernel, task, slots, tile(width, 256)),
        out_shape=jax.ShapeDtypeStruct((high, width), jnp.bfloat16),
        grid_spec=pltpu.PrefetchScalarGridSpec(
            num_scalar_prefetch=1,
            grid=(high // block,),
            in_specs=[
                pl.BlockSpec((devices, 1, tokens_each, block), lambda i, s: (0, task, 0, i)),
                pl.BlockSpec(g.shape, lambda i, s: (0, 0)),
            ],
            out_specs=pl.BlockSpec((block, width), lambda i, s: (i, 0)),
        ),
        compiler_params=pltpu.CompilerParams(vmem_limit_bytes=40 * 1024 * 1024),
        cost_estimate=pl.CostEstimate(
            flops=4 * high * width * g.shape[0], bytes_accessed=2 * high * width, transcendentals=0
        ),
    )(table, x, g)


def merge_kernel(tasks, slots, part, table_ref, *refs):
    f_ref, x_refs, g_refs = refs[0], refs[1:tasks], refs[tasks : 2 * tasks - 1]
    w_refs, out_ref = refs[2 * tasks - 1 : 3 * tasks - 1], refs[-1]
    for start in range(0, out_ref.shape[1], part):
        columns = slice(start, start + part)
        numer, denom = None, None
        for task in range(tasks):
            if task == 0:
                fisher = f_ref[:, columns]
            else:
                fisher = fisher_rows(table_ref, task, x_refs[task - 1], g_refs[task - 1], slots, columns)
            fisher = fisher.astype(jnp.float32)
            term = fisher * w_refs[task][:, columns].astype(jnp.float32)
            numer = term if numer is None else numer + term
            denom = fisher if denom is None else denom + fisher
        out_ref[:, columns] = (numer / (denom + 1e-6)).astype(out_ref.dtype)


def merge_columns(piece, slots, table, fisher, x, g, own, others, merged):
    tasks = 1 + len(others)
    devices, _, tokens_each, _ = x.shape
    high, width = fisher.shape
    some = g[0].shape[1]
    block = tile(high, 512)
    here = pl.BlockSpec((block, some), lambda i, s: (i, piece))
    own_spec = pl.BlockSpec((block, some), lambda i, s: (s[0, s.shape[1] - 1] * (high // block) + i, piece))
    x_specs = [
        pl.BlockSpec((devices, 1, tokens_each, block), functools.partial(lambda t, i, s: (0, t, 0, i), t))
        for t in range(1, tasks)
    ]
    g_specs = [pl.BlockSpec(part.shape, lambda i, s: (0, 0)) for part in g]
    in_specs = [here, *x_specs, *g_specs, own_spec] + [here] * (tasks - 1)
    operands = [table, fisher, *([x] * (tasks - 1)), *g, own, *others]
    aliases = {}
    if merged is not None:
        aliases = {len(operands): 0}
        in_specs.append(pl.BlockSpec(memory_space=pl.ANY))
        operands.append(merged)
    return pl.pallas_call(
        functools.partial(merge_kernel, tasks, slots, tile(some, 256)),
        out_shape=jax.ShapeDtypeStruct((high, width), jnp.bfloat16),
        grid_spec=pltpu.PrefetchScalarGridSpec(
            num_scalar_prefetch=1, grid=(high // block,), in_specs=in_specs, out_specs=here
        ),
        input_output_aliases=aliases,
        compiler_params=pltpu.CompilerParams(vmem_limit_bytes=40 * 1024 * 1024),
        cost_estimate=pl.CostEstimate(
            flops=4 * (tasks - 1) * high * some * g[0].shape[0],
            bytes_accessed=2 * (2 * tasks + 1) * high * some,
            transcendentals=0,
        ),
    )(*operands)


PIECES = 4
LANES = 128


def keep_rows(rows, count, starts, lengths):
    row = lax.axis_index("shard") * rows.shape[0] + jnp.arange(rows.shape[0], dtype=jnp.int32)[:, None]
    slot = jnp.arange(starts.shape[0], dtype=jnp.int32)
    keep = jnp.any((row >= starts) & (row < starts + lengths) & (slot < count), axis=1)
    return jnp.where(keep[:, None], rows, jnp.zeros_like(rows))


def per_device(tasks, acts, cotangents, task_weights, example_count, example_start, example_len):
    slots = example_start.shape[1]
    mine = lax.axis_index("task")
    high = acts.shape[2] // tasks
    steps = range(1, tasks)

    def hand_on(step, value):
        return lax.ppermute(value, "task", [(i, (i + step) % tasks) for i in range(tasks)])

    def block_of(step, value, axis):
        return lax.dynamic_slice_in_dim(value, lax.rem(mine + step, tasks) * high, high, axis)

    own = jnp.concatenate([example_count, mine[None]])
    table = jnp.stack([own] + [hand_on(step, own) for step in steps])

    kept = keep_rows(acts[0], example_count, example_start[0], example_len[0])
    x_parts = [block_of(0, kept, 1)] + [hand_on(step, block_of(step, kept, 1)) for step in steps]
    x = lax.all_gather(jnp.stack(x_parts), "shard", axis=0)
    others = [hand_on(step, block_of(step, task_weights[0], 0)) for step in steps]
    grads = lax.all_to_all(cotangents[0], "shard", split_axis=1, concat_axis=0, tiled=True)
    ready, others = lax.optimization_barrier((grads, others))
    count = max(1, min(PIECES, grads.shape[1] // LANES))
    some = grads.shape[1] // count
    pieces = [
        [hand_on(step, lax.slice_in_dim(ready, p * some, (p + 1) * some, axis=1)) for step in steps]
        for p in range(count)
    ]

    fisher = fisher_of(0, slots, table, x, grads, high)
    merged = None
    for piece in range(count):
        merged = merge_columns(
            piece, slots, table, fisher, x, pieces[piece], task_weights[0], others, merged
        )
    return merged


def solution(mesh):
    in_specs = (
        P("task", "shard", None),
        P("task", "shard", None),
        P("task", None, "shard"),
        P("task"),
        P("task", None),
        P("task", None),
    )
    return jax.shard_map(
        functools.partial(per_device, mesh.shape["task"]),
        mesh=mesh,
        in_specs=in_specs,
        out_specs=P("task", "shard"),
        check_vma=False,
    )
```

time: 217 us -> 190 us (0.88)
  the two profiles are of different devices: /device:TPU:0 before, /device:TPU:10 now
where the time goes in v2:
time: 190 us; the launch traced here: 189 us
  waiting for transfers between devices  108 us (57%)
  Pallas kernels  39.9 us (21%)
  between operations  14.1 us (7%)
  starting transfers between devices  13.9 us (7%)
  local copies, waits for them, and re-layouts  9.93 us (5%)
  other arithmetic  3.57 us (2%)
    ppermute x7, waiting for transfers between devices, hand_on(): lax.ppermute(value, 'task', [(i, (i + step) % tasks) for i in range(tasks)])  97.1 us
    pallas_call x4, Pallas kernels, merge_columns(): pl.pallas_call(functools.partial(merge_kernel, tasks, slots, tile(some, 2...  28.4 us
    pallas_call x1, Pallas kernels, fisher_of(): pl.pallas_call(functools.partial(fisher_kernel, task, slots, tile(width,...  11.5 us
    all_to_all x1, waiting for transfers between devices, per_device(): lax.all_to_all(cotangents[0], 'shard', split_axis=1, concat_axis=0, tiled...  10.5 us
    ppermute x7, starting transfers between devices, hand_on(): lax.ppermute(value, 'task', [(i, (i + step) % tasks) for i in range(tasks)])  7.66 us
    all_to_all x1, starting transfers between devices, per_device(): lax.all_to_all(cotangents[0], 'shard', split_axis=1, concat_axis=0, tiled...  6.24 us
    dynamic_slice x1, local copies, waits for them, and re-layouts, block_of(): lax.dynamic_slice_in_dim(value, lax.rem(mine + step, tasks) * high, high,...  4.79 us
  transfers between devices with their start and end apart: 9, of which 6 were waited for; matrix products, arithmetic and copies ran while one was open for 5% of the time, Pallas kernels for 17%

profile of v2, /device:TPU:10, one launch (start us, length us, event | category | flops | bytes accessed | tf_op | source)
XLA Modules:
  0.0 189.0 jit_solution(1900839761410378761)
XLA Ops:
  7.2 0.7 add_bitcast_fusion
  7.9 0.7 and_reduce_fusion
  8.6 1.1 bitcast_select_fusion
  9.8 1.6 collective-permute-start.1
  11.4 6.5 %collective-permute-done.1 = bf16[64,2048]{1,0:T(8,128)(2,1)S(1)} collective-permute-done((bf16[64,2048]{1,0:T(8,128)(2,1)S(1)}, bf16[64,2048]{1,0:T(8,128)(2,1)S(1)}, u32[]{:S(2)}, u32[]{:S(2)}) %collective-permute-start.1) | collective-permute-done | bytes 262176 | tf_op jit(solution)/shard_map/ppermute | solution.py:132
  18.0 0.8 pad_maximum_fusion
  18.8 4.8 %dynamic-slice_bitcast_fusion = bf16[2048,1024]{1,0:T(8,128)(2,1)} fusion(bf16[1,4096,1024]{2,1,0:T(8,128)(2,1)} %param.8, s32[]{:T(128)S(6)} %select_n.13), kind=kLoop, calls=%fused_computation | loop fusion | bytes 8388612 | tf_op jit(solution)/shard_map/dynamic_slice | solution.py:135
  23.6 1.5 collective-permute-start.2
  25.1 1.2 copy.13
  26.4 2.5 %copy.12 = bf16[64,16,1024]{2,0,1:T(8,128)(2,1)} copy(bf16[64,16,1024]{2,1,0:T(8,128)(2,1)S(1)} %bitcast.35) | data formatting | bytes 4194304 | tf_op jit(solution)/shard_map/all_to_all | solution.py:144
  28.8 6.2 %all-to-all-start = ((bf16[64,16,1024]{2,0,1:T(8,128)(2,1)}), bf16[64,16,1024]{2,0,1:T(8,128)(2,1)S(1)}, u32[]{:S(2)}, u32[]{:S(2)}) async-start(bf16[64,16,1024]{2,0,1:T(8,128)(2,1)} %copy.12), calls=%async_computation | async-start | bytes 4194304 | tf_op jit(solution)/shard_map/all_to_all | solution.py:144
  35.7 79.7 %collective-permute-done = s32[2]{0:T(128)S(1)} collective-permute-done((s32[2]{0:T(128)S(1)}, s32[2]{0:T(128)S(1)}, u32[]{:S(2)}, u32[]{:S(2)}) %collective-permute-start) | collective-permute-done | bytes 40 | tf_op jit(solution)/shard_map/ppermute | solution.py:132
  115.4 10.5 %all-to-all-done = bf16[64,16,1024]{2,0,1:T(8,128)(2,1)S(1)} async-done(((bf16[64,16,1024]{2,0,1:T(8,128)(2,1)}), bf16[64,16,1024]{2,0,1:T(8,128)(2,1)S(1)}, u32[]{:S(2)}, u32[]{:S(2)}) %all-to-all-start) | async-done | bytes 2097184 | tf_op jit(solution)/shard_map/all_to_all | solution.py:144
  125.9 1.4 fusion
  127.3 1.4 collective-permute-start.6
  129.3 1.4 collective-permute-start.4
  131.3 11.5 %shard_map.64.refs_0_ = bf16[2048,1024]{1,0:T(8,128)(2,1)S(1)} custom-call(s32[2,2]{1,0:T(2,128)S(1)} %pad_add_fusion.table_ref, bf16[16,2,64,2048]{3,2,1,0:T(8,128)(2,1)} %bitcast.30, bf16[1024,1024]{1,0:T(8,128)(2,1)S(1)} %bitcast.25), custom_call_target="tpu_custom_call" | custom-call | flops 8589934592 | bytes 4194304 | tf_op jit(solution)/shard_map/pallas_call | solution.py:41
  142.8 7.2 %shard_map.65.refs_5_ = bf16[2048,1024]{1,0:T(8,128)(2,1)} custom-call(s32[2,2]{1,0:T(2,128)S(1)} %pad_add_fusion.table_ref, bf16[2048,1024]{1,0:T(8,128)(2,1)S(1)} %shard_map.64.refs_0_, bf16[16,2,64,2048]{3,2,1,0:T(8,128)(2,1)} %bitcast.31, bf16[1024,256]{1,0:T(8,128)(2,1)} %collective-permute-done.6.refs_2_, bf16[4096,1024]{1,0:T(8,128)(2,1)} %bitcast.26, ...), custom_call_target="tpu_custom_call" | custom-call | flops 2147483648 | bytes 5242880 | tf_op jit(solution)/shard_map/pallas_call | solution.py:98
  150.0 3.6 %collective-permute-done.5.refs_2_ = bf16[1024,256]{1,0:T(8,128)(2,1)} collective-permute-done((bf16[1024,256]{1,0:T(8,128)(2,1)}, bf16[1024,256]{1,0:T(8,128)(2,1)}, u32[]{:S(2)}, u32[]{:S(2)}) %collective-permute-start.5) | collective-permute-done | bytes 524320 | tf_op jit(solution)/shard_map/ppermute | solution.py:132
  153.6 7.2 %shard_map.66.refs_5_ = bf16[2048,1024]{1,0:T(8,128)(2,1)} custom-call(s32[2,2]{1,0:T(2,128)S(1)} %pad_add_fusion.table_ref, bf16[2048,1024]{1,0:T(8,128)(2,1)S(1)} %shard_map.64.refs_0_, bf16[16,2,64,2048]{3,2,1,0:T(8,128)(2,1)} %bitcast.32, bf16[1024,256]{1,0:T(8,128)(2,1)} %collective-permute-done.5.refs_2_, ...), custom_call_target="tpu_custom_call", output_to_operand_aliasing={{}: (6, {})} | custom-call | flops 2147483648 | bytes 5242880 | tf_op jit(solution)/shard_map/pallas_call | solution.py:98
  160.8 3.9 %collective-permute-done.4.refs_2_ = bf16[1024,256]{1,0:T(8,128)(2,1)S(1)} collective-permute-done((bf16[1024,256]{1,0:T(8,128)(2,1)}, bf16[1024,256]{1,0:T(8,128)(2,1)S(1)}, u32[]{:S(2)}, u32[]{:S(2)}) %collective-permute-start.4) | collective-permute-done | bytes 524320 | tf_op jit(solution)/shard_map/ppermute | solution.py:132
  164.7 7.0 %shard_map.67.refs_5_ = bf16[2048,1024]{1,0:T(8,128)(2,1)} custom-call(s32[2,2]{1,0:T(2,128)S(1)} %pad_add_fusion.table_ref, bf16[2048,1024]{1,0:T(8,128)(2,1)S(1)} %shard_map.64.refs_0_, bf16[16,2,64,2048]{3,2,1,0:T(8,128)(2,1)} %bitcast.33, bf16[1024,256]{1,0:T(8,128)(2,1)S(1)} %collective-permute-done.4.refs_2_, ...), custom_call_target="tpu_custom_call", output_to_operand_aliasing={{}: (6, {})} | custom-call | flops 2147483648 | bytes 5242880 | tf_op jit(solution)/shard_map/pallas_call | solution.py:98
  171.7 3.4 %collective-permute-done.3.refs_2_ = bf16[1024,256]{1,0:T(8,128)(2,1)S(1)} collective-permute-done((bf16[1024,256]{1,0:T(8,128)(2,1)}, bf16[1024,256]{1,0:T(8,128)(2,1)S(1)}, u32[]{:S(2)}, u32[]{:S(2)}) %collective-permute-start.3) | collective-permute-done | bytes 524320 | tf_op jit(solution)/shard_map/ppermute | solution.py:132
  175.1 7.0 %shard_map.68 = bf16[2048,1024]{1,0:T(8,128)(2,1)} custom-call(s32[2,2]{1,0:T(2,128)S(1)} %pad_add_fusion.table_ref, bf16[2048,1024]{1,0:T(8,128)(2,1)S(1)} %shard_map.64.refs_0_, bf16[16,2,64,2048]{3,2,1,0:T(8,128)(2,1)} %bitcast.34, bf16[1024,256]{1,0:T(8,128)(2,1)S(1)} %collective-permute-done.3.refs_2_, ...), custom_call_target="tpu_custom_call", output_to_operand_aliasing={{}: (6, {})} | custom-call | flops 2147483648 | bytes 5242880 | tf_op jit(solution)/shard_map/pallas_call | solution.py:98
  (16 shorter events, 2.1 us)
Async XLA Ops:
  6.5 124.8 %all-gather.3.cloned.1.call-start = ((), (), s32[]{:S(2)}) async-start(), calls=%async_computation.1 | async-start | bytes 8912896 | tf_op jit(solution)/shard_map/all_gather | solution.py:142
  9.8 8.1 %collective-permute-start.1 = (bf16[64,2048]{1,0:T(8,128)(2,1)S(1)}, bf16[64,2048]{1,0:T(8,128)(2,1)S(1)}, u32[]{:S(2)}, u32[]{:S(2)}) collective-permute-start(bf16[64,2048]{1,0:T(8,128)(2,1)S(1)} %get-tuple-element.14), channel_id=1, source_target_pairs={{0,16},{16,0},{1,17},{17,1},{2,18},{18,2},{3,19},{19,3},{4,20},{20... | collective-permute-start | bytes 786440 | tf_op jit(solution)/shard_map/ppermute | solution.py:132
  18.8 6.3 %copy-start = (bf16[1,64,16384]{2,1,0:T(8,128)(2,1)S(1)}, bf16[1,64,16384]{2,1,0:T(8,128)(2,1)}, u32[]{:S(2)}) copy-start(bf16[1,64,16384]{2,1,0:T(8,128)(2,1)} %param.7) | copy-start | bytes 6291460
  23.6 102.2 %collective-permute-start.2 = (bf16[2048,1024]{1,0:T(8,128)(2,1)}, bf16[2048,1024]{1,0:T(8,128)(2,1)}, u32[]{:S(2)}, u32[]{:S(2)}) collective-permute-start(bf16[2048,1024]{1,0:T(8,128)(2,1)} %dynamic-slice_bitcast_fusion), channel_id=1, source_target_pairs={{0,16},{16,0},{1,17},{17,1},{2,18},{18,2},{3,19},{19,3},{4,20},{20... | collective-permute-start | bytes 12582920 | tf_op jit(solution)/shard_map/ppermute | solution.py:132
  28.8 97.0 %all-to-all-start = ((bf16[64,16,1024]{2,0,1:T(8,128)(2,1)}), bf16[64,16,1024]{2,0,1:T(8,128)(2,1)S(1)}, u32[]{:S(2)}, u32[]{:S(2)}) async-start(bf16[64,16,1024]{2,0,1:T(8,128)(2,1)} %copy.12), calls=%async_computation | async-start | bytes 4194304 | tf_op jit(solution)/shard_map/all_to_all | solution.py:144
  35.1 80.2 %collective-permute-start = (s32[2]{0:T(128)S(1)}, s32[2]{0:T(128)S(1)}, u32[]{:S(2)}, u32[]{:S(2)}) collective-permute-start(s32[2]{0:T(128)S(1)} %pad_add_fusion.1), channel_id=1, source_target_pairs={{0,16},{16,0},{1,17},{17,1},{2,18},{18,2},{3,19},{19,3},{4,20},{20... | collective-permute-start | bytes 32 | tf_op jit(solution)/shard_map/ppermute | solution.py:132
  127.3 15.5 %collective-permute-start.6 = (bf16[1024,256]{1,0:T(8,128)(2,1)}, bf16[1024,256]{1,0:T(8,128)(2,1)}, u32[]{:S(2)}, u32[]{:S(2)}) collective-permute-start(bf16[1024,256]{1,0:T(8,128)(2,1)} %get-tuple-element.9), channel_id=1, source_target_pairs={{0,16},{16,0},{1,17},{17,1},{2,18},{18,2},{3,19},{19,3},{4,20},{20... | collective-permute-start | bytes 1572872 | tf_op jit(solution)/shard_map/ppermute | solution.py:132
  128.6 25.0 %collective-permute-start.5 = (bf16[1024,256]{1,0:T(8,128)(2,1)}, bf16[1024,256]{1,0:T(8,128)(2,1)}, u32[]{:S(2)}, u32[]{:S(2)}) collective-permute-start(bf16[1024,256]{1,0:T(8,128)(2,1)} %get-tuple-element.10), channel_id=1, source_target_pairs={{0,16},{16,0},{1,17},{17,1},{2,18},{18,2},{3,19},{19,3},{4,20},{20... | collective-permute-start | bytes 1572872 | tf_op jit(solution)/shard_map/ppermute | solution.py:132
  129.3 35.4 %collective-permute-start.4 = (bf16[1024,256]{1,0:T(8,128)(2,1)}, bf16[1024,256]{1,0:T(8,128)(2,1)S(1)}, u32[]{:S(2)}, u32[]{:S(2)}) collective-permute-start(bf16[1024,256]{1,0:T(8,128)(2,1)} %get-tuple-element.11), channel_id=1, source_target_pairs={{0,16},{16,0},{1,17},{17,1},{2,18},{18,2},{3,19},{19,3},{4,20},{20... | collective-permute-start | bytes 1572872 | tf_op jit(solution)/shard_map/ppermute | solution.py:132
  130.7 44.5 %collective-permute-start.3 = (bf16[1024,256]{1,0:T(8,128)(2,1)}, bf16[1024,256]{1,0:T(8,128)(2,1)S(1)}, u32[]{:S(2)}, u32[]{:S(2)}) collective-permute-start(bf16[1024,256]{1,0:T(8,128)(2,1)} %get-tuple-element.12), channel_id=1, source_target_pairs={{0,16},{16,0},{1,17},{17,1},{2,18},{18,2},{3,19},{19,3},{4,20},{20... | collective-permute-start | bytes 1572872 | tf_op jit(solution)/shard_map/ppermute | solution.py:132
Sparse Core Ops, SparseCore 0:
  18.9 105.9 all-gather.2

commit v3 on v2

--- a/solution.py
+++ b/solution.py
@@ -45,7 +45,7 @@
             num_scalar_prefetch=1,
             grid=(high // block,),
             in_specs=[
-                pl.BlockSpec((devices, 1, tokens_each, block), lambda i, s: (0, task, 0, i)),
+                pl.BlockSpec((devices, 1, tokens_each, block), lambda i, s: (0, 0, 0, i)),
                 pl.BlockSpec(g.shape, lambda i, s: (0, 0)),
             ],
             out_specs=pl.BlockSpec((block, width), lambda i, s: (i, 0)),
@@ -77,19 +77,18 @@
 
 def merge_columns(piece, slots, table, fisher, x, g, own, others, merged):
     tasks = 1 + len(others)
-    devices, _, tokens_each, _ = x.shape
+    devices, _, tokens_each, _ = x[0].shape
     high, width = fisher.shape
     some = g[0].shape[1]
     block = tile(high, 512)
     here = pl.BlockSpec((block, some), lambda i, s: (i, piece))
     own_spec = pl.BlockSpec((block, some), lambda i, s: (s[0, s.shape[1] - 1] * (high // block) + i, piece))
     x_specs = [
-        pl.BlockSpec((devices, 1, tokens_each, block), functools.partial(lambda t, i, s: (0, t, 0, i), t))
-        for t in range(1, tasks)
+        pl.BlockSpec((devices, 1, tokens_each, block), lambda i, s: (0, 0, 0, i)) for _ in range(1, tasks)
     ]
     g_specs = [pl.BlockSpec(part.shape, lambda i, s: (0, 0)) for part in g]
     in_specs = [here, *x_specs, *g_specs, own_spec] + [here] * (tasks - 1)
-    operands = [table, fisher, *([x] * (tasks - 1)), *g, own, *others]
+    operands = [table, fisher, *x, *g, own, *others]
     aliases = {}
     if merged is not None:
         aliases = {len(operands): 0}
@@ -111,8 +110,14 @@
     )(*operands)
 
 
-PIECES = 4
 LANES = 128
+
+
+def piece_bounds(width):
+    half, quarter = width // 2, width // 4
+    if quarter % LANES == 0:
+        return [(0, half), (half, half + quarter), (half + quarter, width)]
+    return [(0, half), (half, width)] if half % LANES == 0 else [(0, width)]
 
 
 def keep_rows(rows, count, starts, lengths):
@@ -139,22 +144,22 @@
 
     kept = keep_rows(acts[0], example_count, example_start[0], example_len[0])
     x_parts = [block_of(0, kept, 1)] + [hand_on(step, block_of(step, kept, 1)) for step in steps]
-    x = lax.all_gather(jnp.stack(x_parts), "shard", axis=0)
+    x = [lax.all_gather(part[None], "shard", axis=0) for part in x_parts]
     others = [hand_on(step, block_of(step, task_weights[0], 0)) for step in steps]
-    grads = lax.all_to_all(cotangents[0], "shard", split_axis=1, concat_axis=0, tiled=True)
+    width = task_weights.shape[2]
+    blocks = jnp.stack([cotangents[0][:, i : i + width] for i in range(0, cotangents.shape[2], width)])
+    grads = lax.all_to_all(blocks, "shard", split_axis=0, concat_axis=0, tiled=True).reshape(-1, width)
     ready, others = lax.optimization_barrier((grads, others))
-    count = max(1, min(PIECES, grads.shape[1] // LANES))
-    some = grads.shape[1] // count
+    bounds = piece_bounds(width)
     pieces = [
-        [hand_on(step, lax.slice_in_dim(ready, p * some, (p + 1) * some, axis=1)) for step in steps]
-        for p in range(count)
+        [hand_on(step, lax.slice_in_dim(ready, low, top, axis=1)) for step in steps] for low, top in bounds
     ]
 
-    fisher = fisher_of(0, slots, table, x, grads, high)
+    fisher = fisher_of(0, slots, table, x[0], grads, high)
     merged = None
-    for piece in range(count):
+    for piece, (low, top) in enumerate(bounds):
         merged = merge_columns(
-            piece, slots, table, fisher, x, pieces[piece], task_weights[0], others, merged
+            low // (top - low), slots, table, fisher, x[1:], pieces[piece], task_weights[0], others, merged
         )
     return merged
 

time: 190 us -> 178 us (0.937)
  the two profiles are of different devices: /device:TPU:10 before, /device:TPU:0 now
where the time goes in v3:
time: 178 us
  waiting for transfers between devices  86.5 us (49%)
  Pallas kernels  33 us (19%)
  local copies, waits for them, and re-layouts  27.4 us (15%)
  starting transfers between devices  14.1 us (8%)
  between operations  14.1 us (8%)
  other arithmetic  2.74 us (2%)
    ppermute x6, waiting for transfers between devices, hand_on(): lax.ppermute(value, 'task', [(i, (i + step) % tasks) for i in range(tasks)])  80.4 us
    pallas_call x3, Pallas kernels, merge_columns(): pl.pallas_call(functools.partial(merge_kernel, tasks, slots, tile(some, 2...  22.5 us
    unnamed x27, local copies, waits for them, and re-layouts  19.1 us
    pallas_call x1, Pallas kernels, fisher_of(): pl.pallas_call(functools.partial(fisher_kernel, task, slots, tile(width,...  10.5 us
    ppermute x6, starting transfers between devices, hand_on(): lax.ppermute(value, 'task', [(i, (i + step) % tasks) for i in range(tasks)])  7.72 us
    all_to_all x1, starting transfers between devices, per_device(): lax.all_to_all(blocks, 'shard', split_axis=0, concat_axis=0, tiled=True)  6.32 us
    all_gather x2, waiting for transfers between devices, per_device(): x = [lax.all_gather(part[None], 'shard', axis=0) for part in x_parts]  6.01 us
    dynamic_slice x2, local copies, waits for them, and re-layouts, block_of(): lax.dynamic_slice_in_dim(value, lax.rem(mine + step, tasks) * high, high,...  5.4 us
  transfers between devices with their start and end apart: 9, of which 3 were waited for; matrix products, arithmetic and copies ran while one was open for 10% of the time, Pallas kernels for 15%

profile of v3, /device:TPU:0, one launch (start us, length us, event | category | flops | bytes accessed | tf_op | source)
XLA Modules:
  0.0 177.9 jit_solution(7544757958651703582)
XLA Ops:
  7.9 0.7 and_reduce_fusion
  8.6 1.1 bitcast_select_fusion
  9.8 0.8 constant_dynamic-slice_fusion
  10.6 3.0 %collective-permute-start.1 = (bf16[64,2048]{1,0:T(8,128)(2,1)S(1)}, bf16[64,2048]{1,0:T(8,128)(2,1)S(1)}, u32[]{:S(2)}, u32[]{:S(2)}) collective-permute-start(bf16[64,2048]{1,0:T(8,128)(2,1)S(1)} %get-tuple-element.11), channel_id=1, source_target_pairs={{0,16},{16,0},{1,17},{17,1},{2,18},{18,2},{3,19},{19,3},{4,20},{20... | collective-permute-start | bytes 786440 | tf_op jit(solution)/shard_map/ppermute | solution.py:137
  13.7 4.6 %dynamic-slice_bitcast_fusion = bf16[2048,1024]{1,0:T(8,128)(2,1)} fusion(bf16[1,4096,1024]{2,1,0:T(8,128)(2,1)} %param.8, s32[]{:T(128)S(6)} %select_n.13), kind=kLoop, calls=%fused_computation | loop fusion | bytes 8388612 | tf_op jit(solution)/shard_map/dynamic_slice | solution.py:140
  20.5 0.7 copy-done.5
  29.7 6.3 %all-to-all-start = ((bf16[16,64,1024]{2,1,0:T(8,128)(2,1)}), bf16[16,64,1024]{2,1,0:T(8,128)(2,1)S(1)}, u32[]{:S(2)}, u32[]{:S(2)}) async-start(bf16[16,64,1024]{2,1,0:T(8,128)(2,1)} %fusion), calls=%async_computation | async-start | bytes 4194304 | tf_op jit(solution)/shard_map/all_to_all | solution.py:151
  36.1 1.5 collective-permute-start
  37.7 73.0 %collective-permute-done = s32[2]{0:T(128)S(1)} collective-permute-done((s32[2]{0:T(128)S(1)}, s32[2]{0:T(128)S(1)}, u32[]{:S(2)}, u32[]{:S(2)}) %collective-permute-start) | collective-permute-done | bytes 40 | tf_op jit(solution)/shard_map/ppermute | solution.py:137
  110.7 1.1 slice.75
  111.8 1.0 collective-permute-start.5
  112.9 1.1 fusion.16
  113.9 1.0 collective-permute-start.4
  114.9 1.0 collective-permute-start.3
  116.0 2.2 %copy-done.3 = bf16[1024,2048]{1,0:T(8,128)(2,1)S(1)} copy-done((bf16[1024,2048]{1,0:T(8,128)(2,1)S(1)}, bf16[1024,2048]{1,0:T(8,128)(2,1)}, u32[]{:S(2)}) %copy-start.3) | copy-done | bytes 4194328
  118.2 10.5 %shard_map.64.refs_0_ = bf16[2048,1024]{1,0:T(8,128)(2,1)S(1)} custom-call(s32[2,2]{1,0:T(2,128)S(1)} %pad_add_fusion.table_ref, bf16[16,1,64,2048]{3,2,1,0:T(8,128)(2,1)S(1)} %bitcast.88, bf16[1024,1024]{1,0:T(8,128)(2,1)S(1)} %bitcast.87), custom_call_target="tpu_custom_call" | custom-call | flops 8589934592 | bytes 4194304 | tf_op jit(solution)/shard_map/pallas_call | solution.py:41
  128.7 2.0 %copy-done.1 = bf16[2048,1024]{1,0:T(8,128)(2,1)} copy-done((bf16[2048,1024]{1,0:T(8,128)(2,1)}, bf16[2048,1024]{1,0:T(8,128)(2,1)S(1)}, u32[]{:S(2)}) %copy-start.1) | copy-done | bytes 4194328
  130.7 7.5 %collective-permute-done.5.refs_2_ = bf16[1024,512]{1,0:T(8,128)(2,1)S(1)} collective-permute-done((bf16[1024,512]{1,0:T(8,128)(2,1)}, bf16[1024,512]{1,0:T(8,128)(2,1)S(1)}, u32[]{:S(2)}, u32[]{:S(2)}) %collective-permute-start.5) | collective-permute-done | bytes 1048608 | tf_op jit(solution)/shard_map/ppermute | solution.py:137
  138.1 6.0 %all-gather.7.cloned.1.call-done = bf16[1024,2048]{1,0:T(8,128)(2,1)} async-done(((bf16[64,2048]{1,0:T(8,128)(2,1)}), bf16[1024,2048]{1,0:T(8,128)(2,1)}) %all-gather.7.cloned.1.call-update) | async-done | bytes 4194320 | tf_op jit(solution)/shard_map/all_gather | solution.py:147
  144.1 2.2 %copy-done = bf16[1024,2048]{1,0:T(8,128)(2,1)S(1)} copy-done((bf16[1024,2048]{1,0:T(8,128)(2,1)S(1)}, bf16[1024,2048]{1,0:T(8,128)(2,1)}, u32[]{:S(2)}) %copy-start) | copy-done | bytes 4194328
  146.3 2.2 %copy-done.2 = bf16[2048,1024]{1,0:T(8,128)(2,1)S(1)} copy-done((bf16[2048,1024]{1,0:T(8,128)(2,1)S(1)}, bf16[2048,1024]{1,0:T(8,128)(2,1)}, u32[]{:S(2)}) %copy-start.2) | copy-done | bytes 4194328
  148.5 9.3 %shard_map.65.refs_5_ = bf16[2048,1024]{1,0:T(8,128)(2,1)} custom-call(s32[2,2]{1,0:T(2,128)S(1)} %pad_add_fusion.table_ref, bf16[2048,1024]{1,0:T(8,128)(2,1)S(1)} %copy-done.2, bf16[16,1,64,2048]{3,2,1,0:T(8,128)(2,1)S(1)} %bitcast.82, bf16[1024,512]{1,0:T(8,128)(2,1)S(1)} %collective-permute-done.5.refs_2_, bf16[4096,1024]{1,0:T(8,128)(2,1)} %bitcast.89, ...), custom_call_target="tpu_custom_call" | custom-call | flops 4294967296 | bytes 10485760 | tf_op jit(solution)/shard_map/pallas_call | solution.py:97
  157.8 6.6 %shard_map.66.refs_5_ = bf16[2048,1024]{1,0:T(8,128)(2,1)} custom-call(s32[2,2]{1,0:T(2,128)S(1)} %pad_add_fusion.table_ref, bf16[2048,1024]{1,0:T(8,128)(2,1)S(1)} %copy-done.2, bf16[16,1,64,2048]{3,2,1,0:T(8,128)(2,1)S(1)} %bitcast.83, bf16[1024,256]{1,0:T(8,128)(2,1)} %collective-permute-done.4.refs_2_, ...), custom_call_target="tpu_custom_call", output_to_operand_aliasing={{}: (6, {})} | custom-call | flops 2147483648 | bytes 5242880 | tf_op jit(solution)/shard_map/pallas_call | solution.py:97
  164.4 6.6 %shard_map.67 = bf16[2048,1024]{1,0:T(8,128)(2,1)} custom-call(s32[2,2]{1,0:T(2,128)S(1)} %pad_add_fusion.table_ref, bf16[2048,1024]{1,0:T(8,128)(2,1)S(1)} %copy-done.2, bf16[16,1,64,2048]{3,2,1,0:T(8,128)(2,1)S(1)} %bitcast.84, bf16[1024,256]{1,0:T(8,128)(2,1)} %collective-permute-done.3.refs_2_, ...), custom_call_target="tpu_custom_call", output_to_operand_aliasing={{}: (6, {})} | custom-call | flops 2147483648 | bytes 5242880 | tf_op jit(solution)/shard_map/pallas_call | solution.py:97
  (40 shorter events, 11.6 us)
Async XLA Ops:
  6.5 109.4 %all-gather.5.cloned.1.call-start = ((), (), s32[]{:S(2)}) async-start(), calls=%async_computation.1 | async-start | bytes 4456448 | tf_op jit(solution)/shard_map/all_gather | solution.py:147
  10.6 133.6 %all-gather.7.cloned.1.call-start = ((), (), s32[]{:S(2)}) async-start(), calls=%async_computation.2 | async-start | bytes 4456448 | tf_op jit(solution)/shard_map/all_gather | solution.py:147
  10.6 7.8 %copy-start.4 = (bf16[1,64,16384]{2,1,0:T(8,128)(2,1)S(1)}, bf16[1,64,16384]{2,1,0:T(8,128)(2,1)}, u32[]{:S(2)}) copy-start(bf16[1,64,16384]{2,1,0:T(8,128)(2,1)} %param.7) | copy-start | bytes 6291460
  10.6 9.8 %collective-permute-start.1 = (bf16[64,2048]{1,0:T(8,128)(2,1)S(1)}, bf16[64,2048]{1,0:T(8,128)(2,1)S(1)}, u32[]{:S(2)}, u32[]{:S(2)}) collective-permute-start(bf16[64,2048]{1,0:T(8,128)(2,1)S(1)} %get-tuple-element.11), channel_id=1, source_target_pairs={{0,16},{16,0},{1,17},{17,1},{2,18},{18,2},{3,19},{19,3},{4,20},{20... | collective-permute-start | bytes 786440 | tf_op jit(solution)/shard_map/ppermute | solution.py:137
  18.3 92.4 %collective-permute-start.2 = (bf16[2048,1024]{1,0:T(8,128)(2,1)}, bf16[2048,1024]{1,0:T(8,128)(2,1)}, u32[]{:S(2)}, u32[]{:S(2)}) collective-permute-start(bf16[2048,1024]{1,0:T(8,128)(2,1)} %dynamic-slice_bitcast_fusion), channel_id=1, source_target_pairs={{0,16},{16,0},{1,17},{17,1},{2,18},{18,2},{3,19},{19,3},{4,20},{20... | collective-permute-start | bytes 12582920 | tf_op jit(solution)/shard_map/ppermute | solution.py:137
  20.5 0.7 copy-start.5
  29.7 80.9 %all-to-all-start = ((bf16[16,64,1024]{2,1,0:T(8,128)(2,1)}), bf16[16,64,1024]{2,1,0:T(8,128)(2,1)S(1)}, u32[]{:S(2)}, u32[]{:S(2)}) async-start(bf16[16,64,1024]{2,1,0:T(8,128)(2,1)} %fusion), calls=%async_computation | async-start | bytes 4194304 | tf_op jit(solution)/shard_map/all_to_all | solution.py:151
  36.1 74.5 %collective-permute-start = (s32[2]{0:T(128)S(1)}, s32[2]{0:T(128)S(1)}, u32[]{:S(2)}, u32[]{:S(2)}) collective-permute-start(s32[2]{0:T(128)S(1)} %pad_add_fusion.1), channel_id=1, source_target_pairs={{0,16},{16,0},{1,17},{17,1},{2,18},{18,2},{3,19},{19,3},{4,20},{20... | collective-permute-start | bytes 32 | tf_op jit(solution)/shard_map/ppermute | solution.py:137
  111.8 26.3 %collective-permute-start.5 = (bf16[1024,512]{1,0:T(8,128)(2,1)}, bf16[1024,512]{1,0:T(8,128)(2,1)S(1)}, u32[]{:S(2)}, u32[]{:S(2)}) collective-permute-start(bf16[1024,512]{1,0:T(8,128)(2,1)} %slice.75), channel_id=1, source_target_pairs={{0,16},{16,0},{1,17},{17,1},{2,18},{18,2},{3,19},{19,3},{4,20},{20... | collective-permute-start | bytes 3145736 | tf_op jit(solution)/shard_map/ppermute | solution.py:137
  113.9 43.8 %collective-permute-start.4 = (bf16[1024,256]{1,0:T(8,128)(2,1)}, bf16[1024,256]{1,0:T(8,128)(2,1)}, u32[]{:S(2)}, u32[]{:S(2)}) collective-permute-start(bf16[1024,256]{1,0:T(8,128)(2,1)} %get-tuple-element.9), channel_id=1, source_target_pairs={{0,16},{16,0},{1,17},{17,1},{2,18},{18,2},{3,19},{19,3},{4,20},{20... | collective-permute-start | bytes 1572872 | tf_op jit(solution)/shard_map/ppermute | solution.py:137
  114.9 49.5 %collective-permute-start.3 = (bf16[1024,256]{1,0:T(8,128)(2,1)}, bf16[1024,256]{1,0:T(8,128)(2,1)}, u32[]{:S(2)}, u32[]{:S(2)}) collective-permute-start(bf16[1024,256]{1,0:T(8,128)(2,1)} %get-tuple-element.10), channel_id=1, source_target_pairs={{0,16},{16,0},{1,17},{17,1},{2,18},{18,2},{3,19},{19,3},{4,20},{20... | collective-permute-start | bytes 1572872 | tf_op jit(solution)/shard_map/ppermute | solution.py:137
  116.0 2.2 %copy-start.3 = (bf16[1024,2048]{1,0:T(8,128)(2,1)S(1)}, bf16[1024,2048]{1,0:T(8,128)(2,1)}, u32[]{:S(2)}) copy-start(bf16[1024,2048]{1,0:T(8,128)(2,1)} %all-gather.5.cloned.1.call-done) | copy-start | bytes 12582916
  128.6 2.0 %copy-start.1 = (bf16[2048,1024]{1,0:T(8,128)(2,1)}, bf16[2048,1024]{1,0:T(8,128)(2,1)S(1)}, u32[]{:S(2)}) copy-start(bf16[2048,1024]{1,0:T(8,128)(2,1)S(1)} %shard_map.64.refs_0_) | copy-start | bytes 12582916
  144.1 2.2 %copy-start = (bf16[1024,2048]{1,0:T(8,128)(2,1)S(1)}, bf16[1024,2048]{1,0:T(8,128)(2,1)}, u32[]{:S(2)}) copy-start(bf16[1024,2048]{1,0:T(8,128)(2,1)} %all-gather.7.cloned.1.call-done) | copy-start | bytes 12582916
  146.3 2.2 %copy-start.2 = (bf16[2048,1024]{1,0:T(8,128)(2,1)S(1)}, bf16[2048,1024]{1,0:T(8,128)(2,1)}, u32[]{:S(2)}) copy-start(bf16[2048,1024]{1,0:T(8,128)(2,1)} %copy-done.1) | copy-start | bytes 12582916
Sparse Core Ops, SparseCore 0:
  10.7 79.8 all-gather.4
  92.8 51.3 all-gather.6

commit v4 on v3

--- a/solution.py
+++ b/solution.py
@@ -57,9 +57,11 @@
     )(table, x, g)
 
 
-def merge_kernel(tasks, slots, part, table_ref, *refs):
-    f_ref, x_refs, g_refs = refs[0], refs[1:tasks], refs[tasks : 2 * tasks - 1]
-    w_refs, out_ref = refs[2 * tasks - 1 : 3 * tasks - 1], refs[-1]
+def merge_kernel(tasks, slots, part, joined, table_ref, *refs):
+    f_ref, x_refs, refs = refs[0], refs[1:tasks], refs[tasks:]
+    g_refs, refs = refs[: joined * (tasks - 1)], refs[joined * (tasks - 1) :]
+    w_refs, out_ref = refs[:tasks], refs[-1]
+    where = [(i, at) for i in range(joined) for at in range(0, g_refs[i].shape[1], part)]
     for start in range(0, out_ref.shape[1], part):
         columns = slice(start, start + part)
         numer, denom = None, None
@@ -67,7 +69,9 @@
             if task == 0:
                 fisher = f_ref[:, columns]
             else:
-                fisher = fisher_rows(table_ref, task, x_refs[task - 1], g_refs[task - 1], slots, columns)
+                piece, at = where[start // part]
+                g_ref = g_refs[(task - 1) * joined + piece]
+                fisher = fisher_rows(table_ref, task, x_refs[task - 1], g_ref, slots, slice(at, at + part))
             fisher = fisher.astype(jnp.float32)
             term = fisher * w_refs[task][:, columns].astype(jnp.float32)
             numer = term if numer is None else numer + term
@@ -79,7 +83,8 @@
     tasks = 1 + len(others)
     devices, _, tokens_each, _ = x[0].shape
     high, width = fisher.shape
-    some = g[0].shape[1]
+    joined = len(g) // (tasks - 1)
+    some = sum(part.shape[1] for part in g[:joined])
     block = tile(high, 512)
     here = pl.BlockSpec((block, some), lambda i, s: (i, piece))
     own_spec = pl.BlockSpec((block, some), lambda i, s: (s[0, s.shape[1] - 1] * (high // block) + i, piece))
@@ -95,13 +100,13 @@
         in_specs.append(pl.BlockSpec(memory_space=pl.ANY))
         operands.append(merged)
     return pl.pallas_call(
-        functools.partial(merge_kernel, tasks, slots, tile(some, 256)),
+        functools.partial(merge_kernel, tasks, slots, min(tile(part.shape[1], 256) for part in g), joined),
         out_shape=jax.ShapeDtypeStruct((high, width), jnp.bfloat16),
         grid_spec=pltpu.PrefetchScalarGridSpec(
             num_scalar_prefetch=1, grid=(high // block,), in_specs=in_specs, out_specs=here
         ),
         input_output_aliases=aliases,
-        compiler_params=pltpu.CompilerParams(vmem_limit_bytes=40 * 1024 * 1024),
+        compiler_params=pltpu.CompilerParams(vmem_limit_bytes=60 * 1024 * 1024),
         cost_estimate=pl.CostEstimate(
             flops=4 * (tasks - 1) * high * some * g[0].shape[0],
             bytes_accessed=2 * (2 * tasks + 1) * high * some,
@@ -157,9 +162,12 @@
 
     fisher = fisher_of(0, slots, table, x[0], grads, high)
     merged = None
-    for piece, (low, top) in enumerate(bounds):
+    groups = [range(0, 2), range(2, 3)] if len(bounds) == 3 else [[p] for p in range(len(bounds))]
+    for group in groups:
+        low, top = bounds[group[0]][0], bounds[group[-1]][1]
+        g = [pieces[p][step - 1] for step in steps for p in group]
         merged = merge_columns(
-            low // (top - low), slots, table, fisher, x[1:], pieces[piece], task_weights[0], others, merged
+            low // (top - low), slots, table, fisher, x[1:], g, task_weights[0], others, merged
         )
     return merged
 

time: 178 us -> 177 us (level)
  local copies, waits for them, and re-layouts: 27.4 us -> 22.1 us
  waiting for transfers between devices: 86.5 us -> 91.6 us
    ppermute x6, waiting for transfers between devices: 80.4 us -> 91.5 us  [hand_on(): lax.ppermute(value, 'task', [(i, (i + step) % tasks) for i in range(tasks)])]
    all_gather x2, waiting for transfers between devices: 6.01 us -> 0.01 us  [per_device(): x = [lax.all_gather(part[None], 'shard', axis=0) for part in x_parts]]
    unnamed x27 -> x25, local copies, waits for them, and re-layouts: 19.1 us -> 14.8 us
    pallas_call x3 -> x2, Pallas kernels: 22.5 us -> 21.3 us  [merge_columns(): pl.pallas_call(functools.partial(merge_kernel, tasks, slots, min((tile(pa...]
  transfers between devices with their start and end apart: 9 -> 9, of which waited for: 3 -> 2; matrix products, arithmetic and copies ran while one was open for 10% -> 9% of each run, Pallas kernels for 15% -> 14%
where the time goes in v4:
time: 177 us; the launch traced here: 176 us
  waiting for transfers between devices  91.6 us (52%)
  Pallas kernels  31.7 us (18%)
  local copies, waits for them, and re-layouts  22.1 us (12%)
  between operations  14.2 us (8%)
  starting transfers between devices  14.1 us (8%)
  other arithmetic  2.74 us (2%)
    ppermute x6, waiting for transfers between devices, hand_on(): lax.ppermute(value, 'task', [(i, (i + step) % tasks) for i in range(tasks)])  91.5 us
    pallas_call x2, Pallas kernels, merge_columns(): pl.pallas_call(functools.partial(merge_kernel, tasks, slots, min((tile(pa...  21.3 us
    unnamed x25, local copies, waits for them, and re-layouts  14.8 us
    pallas_call x1, Pallas kernels, fisher_of(): pl.pallas_call(functools.partial(fisher_kernel, task, slots, tile(width,...  10.5 us
    ppermute x6, starting transfers between devices, hand_on(): lax.ppermute(value, 'task', [(i, (i + step) % tasks) for i in range(tasks)])  7.79 us
    all_to_all x1, starting transfers between devices, per_device(): lax.all_to_all(blocks, 'shard', split_axis=0, concat_axis=0, tiled=True)  6.32 us
    dynamic_slice x2, local copies, waits for them, and re-layouts, block_of(): lax.dynamic_slice_in_dim(value, lax.rem(mine + step, tasks) * high, high,...  5.41 us
  transfers between devices with their start and end apart: 9, of which 2 were waited for; matrix products, arithmetic and copies ran while one was open for 9% of the time, Pallas kernels for 14%

profile of v4, /device:TPU:0, one launch (start us, length us, event | category | flops | bytes accessed | tf_op | source)
XLA Modules:
  0.0 176.4 jit_solution(17497734236601237416)
XLA Ops:
  7.2 0.7 add_bitcast_fusion
  7.9 0.7 and_reduce_fusion
  8.6 1.1 bitcast_select_fusion
  9.8 0.8 constant_dynamic-slice_fusion
  10.6 3.0 %collective-permute-start.1 = (bf16[64,2048]{1,0:T(8,128)(2,1)S(1)}, bf16[64,2048]{1,0:T(8,128)(2,1)S(1)}, u32[]{:S(2)}, u32[]{:S(2)}) collective-permute-start(bf16[64,2048]{1,0:T(8,128)(2,1)S(1)} %get-tuple-element.11), channel_id=1, source_target_pairs={{0,16},{16,0},{1,17},{17,1},{2,18},{18,2},{3,19},{19,3},{4,20},{20... | collective-permute-start | bytes 786440 | tf_op jit(solution)/shard_map/ppermute | solution.py:142
  13.7 4.6 %dynamic-slice_bitcast_fusion = bf16[2048,1024]{1,0:T(8,128)(2,1)} fusion(bf16[1,4096,1024]{2,1,0:T(8,128)(2,1)} %param.8, s32[]{:T(128)S(6)} %select_n.13), kind=kLoop, calls=%fused_computation | loop fusion | bytes 8388612 | tf_op jit(solution)/shard_map/dynamic_slice | solution.py:145
  20.5 0.7 copy-done.4
  21.9 0.7 fusion.11
  23.9 0.7 fusion.8
  25.9 0.7 fusion.5
  29.2 0.7 fusion
  29.9 6.3 %all-to-all-start = ((bf16[16,64,1024]{2,1,0:T(8,128)(2,1)}), bf16[16,64,1024]{2,1,0:T(8,128)(2,1)S(1)}, u32[]{:S(2)}, u32[]{:S(2)}) async-start(bf16[16,64,1024]{2,1,0:T(8,128)(2,1)} %fusion), calls=%async_computation | async-start | bytes 4194304 | tf_op jit(solution)/shard_map/all_to_all | solution.py:156
  36.3 1.5 collective-permute-start
  37.8 72.9 %collective-permute-done = s32[2]{0:T(128)S(1)} collective-permute-done((s32[2]{0:T(128)S(1)}, s32[2]{0:T(128)S(1)}, u32[]{:S(2)}, u32[]{:S(2)}) %collective-permute-start) | collective-permute-done | bytes 40 | tf_op jit(solution)/shard_map/ppermute | solution.py:142
  110.8 1.1 collective-permute-start.4
  111.9 1.1 fusion.16
  113.0 1.0 collective-permute-start.5
  114.0 1.0 collective-permute-start.3
  115.0 2.2 %copy-done.2 = bf16[1024,2048]{1,0:T(8,128)(2,1)S(1)} copy-done((bf16[1024,2048]{1,0:T(8,128)(2,1)S(1)}, bf16[1024,2048]{1,0:T(8,128)(2,1)}, u32[]{:S(2)}) %copy-start.2) | copy-done | bytes 4194328
  117.2 10.5 %shard_map.64.refs_0_ = bf16[2048,1024]{1,0:T(8,128)(2,1)S(1)} custom-call(s32[2,2]{1,0:T(2,128)S(1)} %pad_add_fusion.table_ref, bf16[16,1,64,2048]{3,2,1,0:T(8,128)(2,1)S(1)} %bitcast.85, bf16[1024,1024]{1,0:T(8,128)(2,1)S(1)} %bitcast.84), custom_call_target="tpu_custom_call" | custom-call | flops 8589934592 | bytes 4194304 | tf_op jit(solution)/shard_map/pallas_call | solution.py:41
  127.7 2.0 %copy-done = bf16[2048,1024]{1,0:T(8,128)(2,1)} copy-done((bf16[2048,1024]{1,0:T(8,128)(2,1)}, bf16[2048,1024]{1,0:T(8,128)(2,1)S(1)}, u32[]{:S(2)}) %copy-start) | copy-done | bytes 4194328
  129.7 18.7 %collective-permute-done.5.refs_3_ = bf16[1024,256]{1,0:T(8,128)(2,1)} collective-permute-done((bf16[1024,256]{1,0:T(8,128)(2,1)}, bf16[1024,256]{1,0:T(8,128)(2,1)}, u32[]{:S(2)}, u32[]{:S(2)}) %collective-permute-start.5) | collective-permute-done | bytes 524320 | tf_op jit(solution)/shard_map/ppermute | solution.py:142
  148.3 13.4 %shard_map.65.refs_5_ = bf16[2048,1024]{1,0:T(8,128)(2,1)} custom-call(s32[2,2]{1,0:T(2,128)} %copy-done.1, bf16[2048,1024]{1,0:T(8,128)(2,1)} %copy-done, bf16[16,1,64,2048]{3,2,1,0:T(8,128)(2,1)} %bitcast.88, bf16[1024,512]{1,0:T(8,128)(2,1)} %collective-permute-done.4.refs_2_, bf16[1024,256]{1,0:T(8,128)(2,1)} %collective-permute-done.5.refs_3_, ...), custom_call_target="tpu_custom_call" | custom-call | flops 6442450944 | bytes 15728640 | tf_op jit(solution)/shard_map/pallas_call | solution.py:102
  161.7 7.9 %shard_map.66 = bf16[2048,1024]{1,0:T(8,128)(2,1)} custom-call(s32[2,2]{1,0:T(2,128)} %copy-done.1, bf16[2048,1024]{1,0:T(8,128)(2,1)} %copy-done, bf16[16,1,64,2048]{3,2,1,0:T(8,128)(2,1)} %bitcast.89, bf16[1024,256]{1,0:T(8,128)(2,1)} %collective-permute-done.3.refs_2_, bf16[4096,1024]{1,0:T(8,128)(2,1)} %bitcast.87, ...), custom_call_target="tpu_custom_call", output_to_operand_aliasing={{}: (6, {})} | custom-call | flops 2147483648 | bytes 5242880 | tf_op jit(solution)/shard_map/pallas_call | solution.py:102
  (37 shorter events, 8.5 us)
Async XLA Ops:
  6.5 108.5 %all-gather.5.cloned.1.call-start = ((), (), s32[]{:S(2)}) async-start(), calls=%async_computation.1 | async-start | bytes 4456448 | tf_op jit(solution)/shard_map/all_gather | solution.py:152
  10.6 137.7 %all-gather.7.cloned.1.call-start = ((), (), s32[]{:S(2)}) async-start(), calls=%async_computation.2 | async-start | bytes 4456448 | tf_op jit(solution)/shard_map/all_gather | solution.py:152
  10.6 7.8 %copy-start.3 = (bf16[1,64,16384]{2,1,0:T(8,128)(2,1)S(1)}, bf16[1,64,16384]{2,1,0:T(8,128)(2,1)}, u32[]{:S(2)}) copy-start(bf16[1,64,16384]{2,1,0:T(8,128)(2,1)} %param.7) | copy-start | bytes 6291460
  10.6 9.8 %collective-permute-start.1 = (bf16[64,2048]{1,0:T(8,128)(2,1)S(1)}, bf16[64,2048]{1,0:T(8,128)(2,1)S(1)}, u32[]{:S(2)}, u32[]{:S(2)}) collective-permute-start(bf16[64,2048]{1,0:T(8,128)(2,1)S(1)} %get-tuple-element.11), channel_id=1, source_target_pairs={{0,16},{16,0},{1,17},{17,1},{2,18},{18,2},{3,19},{19,3},{4,20},{20... | collective-permute-start | bytes 786440 | tf_op jit(solution)/shard_map/ppermute | solution.py:142
  18.3 92.4 %collective-permute-start.2 = (bf16[2048,1024]{1,0:T(8,128)(2,1)}, bf16[2048,1024]{1,0:T(8,128)(2,1)}, u32[]{:S(2)}, u32[]{:S(2)}) collective-permute-start(bf16[2048,1024]{1,0:T(8,128)(2,1)} %dynamic-slice_bitcast_fusion), channel_id=1, source_target_pairs={{0,16},{16,0},{1,17},{17,1},{2,18},{18,2},{3,19},{19,3},{4,20},{20... | collective-permute-start | bytes 12582920 | tf_op jit(solution)/shard_map/ppermute | solution.py:142
  20.5 0.7 copy-start.4
  29.9 80.8 %all-to-all-start = ((bf16[16,64,1024]{2,1,0:T(8,128)(2,1)}), bf16[16,64,1024]{2,1,0:T(8,128)(2,1)S(1)}, u32[]{:S(2)}, u32[]{:S(2)}) async-start(bf16[16,64,1024]{2,1,0:T(8,128)(2,1)} %fusion), calls=%async_computation | async-start | bytes 4194304 | tf_op jit(solution)/shard_map/all_to_all | solution.py:156
  36.3 74.4 %collective-permute-start = (s32[2]{0:T(128)S(1)}, s32[2]{0:T(128)S(1)}, u32[]{:S(2)}, u32[]{:S(2)}) collective-permute-start(s32[2]{0:T(128)S(1)} %pad_add_fusion.1), channel_id=1, source_target_pairs={{0,16},{16,0},{1,17},{17,1},{2,18},{18,2},{3,19},{19,3},{4,20},{20... | collective-permute-start | bytes 32 | tf_op jit(solution)/shard_map/ppermute | solution.py:142
  110.7 4.3 %copy-start.1 = (s32[2,2]{1,0:T(2,128)}, s32[2,2]{1,0:T(2,128)S(1)}, u32[]{:S(2)}) copy-start(s32[2,2]{1,0:T(2,128)S(1)} %pad_add_fusion.table_ref) | copy-start | bytes 52
  110.8 37.5 %collective-permute-start.4 = (bf16[1024,512]{1,0:T(8,128)(2,1)S(1)}, bf16[1024,512]{1,0:T(8,128)(2,1)}, u32[]{:S(2)}, u32[]{:S(2)}) collective-permute-start(bf16[1024,512]{1,0:T(8,128)(2,1)S(1)} %slice.74), channel_id=1, source_target_pairs={{0,16},{16,0},{1,17},{17,1},{2,18},{18,2},{3,19},{19,3},{4,20},{20... | collective-permute-start | bytes 3145736 | tf_op jit(solution)/shard_map/ppermute | solution.py:142
  113.0 35.3 %collective-permute-start.5 = (bf16[1024,256]{1,0:T(8,128)(2,1)}, bf16[1024,256]{1,0:T(8,128)(2,1)}, u32[]{:S(2)}, u32[]{:S(2)}) collective-permute-start(bf16[1024,256]{1,0:T(8,128)(2,1)} %get-tuple-element.9), channel_id=1, source_target_pairs={{0,16},{16,0},{1,17},{17,1},{2,18},{18,2},{3,19},{19,3},{4,20},{20... | collective-permute-start | bytes 1572872 | tf_op jit(solution)/shard_map/ppermute | solution.py:142
  114.0 47.8 %collective-permute-start.3 = (bf16[1024,256]{1,0:T(8,128)(2,1)}, bf16[1024,256]{1,0:T(8,128)(2,1)}, u32[]{:S(2)}, u32[]{:S(2)}) collective-permute-start(bf16[1024,256]{1,0:T(8,128)(2,1)} %get-tuple-element.10), channel_id=1, source_target_pairs={{0,16},{16,0},{1,17},{17,1},{2,18},{18,2},{3,19},{19,3},{4,20},{20... | collective-permute-start | bytes 1572872 | tf_op jit(solution)/shard_map/ppermute | solution.py:142
  115.0 2.2 %copy-start.2 = (bf16[1024,2048]{1,0:T(8,128)(2,1)S(1)}, bf16[1024,2048]{1,0:T(8,128)(2,1)}, u32[]{:S(2)}) copy-start(bf16[1024,2048]{1,0:T(8,128)(2,1)} %all-gather.5.cloned.1.call-done) | copy-start | bytes 12582916
  127.7 2.0 %copy-start = (bf16[2048,1024]{1,0:T(8,128)(2,1)}, bf16[2048,1024]{1,0:T(8,128)(2,1)S(1)}, u32[]{:S(2)}) copy-start(bf16[2048,1024]{1,0:T(8,128)(2,1)S(1)} %shard_map.64.refs_0_) | copy-start | bytes 12582916
Sparse Core Ops, SparseCore 0:
  10.7 79.9 all-gather.4
  92.9 51.2 all-gather.6

commit v5 on v4

--- a/solution.py
+++ b/solution.py
@@ -15,17 +15,28 @@
     return part
 
 
-def fisher_rows(table_ref, task, x_ref, g_ref, slots, columns):
-    devices, _, rows_each, width = x_ref.shape
+def fisher_tile(table_ref, task, x_ref, g_ref, slots, lanes, columns):
+    devices, _, rows_each, _ = x_ref.shape
     per_slot = rows_each * devices // slots
     spread = devices // slots
     total = None
     for slot in range(slots):
-        x = x_ref[slot * spread : (slot + 1) * spread, 0].reshape(per_slot, width)
+        x = x_ref[slot * spread : (slot + 1) * spread, 0, :, lanes]
+        x = x.reshape(per_slot, x.shape[-1])
         g = g_ref[slot * per_slot : (slot + 1) * per_slot, columns]
         grad = lax.dot_general(x, g, (((0,), (0,)), ((), ())), preferred_element_type=jnp.float32)
         total = grad * grad if total is None else total + grad * grad
     return (total / table_ref[task, 0].astype(jnp.float32)).astype(jnp.bfloat16)
+
+
+def fisher_rows(table_ref, task, x_ref, g_ref, slots, columns):
+    width = x_ref.shape[3]
+    some = tile(width, 128)
+    parts = [
+        fisher_tile(table_ref, task, x_ref, g_ref, slots, slice(low, low + some), columns)
+        for low in range(0, width, some)
+    ]
+    return jnp.concatenate(parts, axis=0)
 
 
 def fisher_kernel(task, slots, part, table_ref, x_ref, g_ref, out_ref):
@@ -85,7 +96,7 @@
     high, width = fisher.shape
     joined = len(g) // (tasks - 1)
     some = sum(part.shape[1] for part in g[:joined])
-    block = tile(high, 512)
+    block = tile(high, 512 if joined > 1 else 1024)
     here = pl.BlockSpec((block, some), lambda i, s: (i, piece))
     own_spec = pl.BlockSpec((block, some), lambda i, s: (s[0, s.shape[1] - 1] * (high // block) + i, piece))
     x_specs = [

time: 177 us -> 175 us (0.989)
  transfers between devices with their start and end apart: 9 -> 9, of which waited for: 2 -> 2; matrix products, arithmetic and copies ran while one was open for 9% -> 9% of each run, Pallas kernels for 14% -> 13%
where the time goes in v5:
time: 175 us
  waiting for transfers between devices  91.5 us (52%)
  Pallas kernels  30.2 us (17%)
  local copies, waits for them, and re-layouts  22.1 us (13%)
  between operations  14.2 us (8%)
  starting transfers between devices  14.1 us (8%)
  other arithmetic  2.74 us (2%)
    ppermute x6, waiting for transfers between devices, hand_on(): lax.ppermute(value, 'task', [(i, (i + step) % tasks) for i in range(tasks)])  91.5 us
    pallas_call x2, Pallas kernels, merge_columns(): pl.pallas_call(functools.partial(merge_kernel, tasks, slots, min((tile(pa...  19.7 us
    unnamed x25, local copies, waits for them, and re-layouts  14.8 us
    pallas_call x1, Pallas kernels, fisher_of(): pl.pallas_call(functools.partial(fisher_kernel, task, slots, tile(width,...  10.5 us
    ppermute x6, starting transfers between devices, hand_on(): lax.ppermute(value, 'task', [(i, (i + step) % tasks) for i in range(tasks)])  7.79 us
    all_to_all x1, starting transfers between devices, per_device(): lax.all_to_all(blocks, 'shard', split_axis=0, concat_axis=0, tiled=True)  6.32 us
    dynamic_slice x2, local copies, waits for them, and re-layouts, block_of(): lax.dynamic_slice_in_dim(value, lax.rem(mine + step, tasks) * high, high,...  5.41 us
  transfers between devices with their start and end apart: 9, of which 2 were waited for; matrix products, arithmetic and copies ran while one was open for 9% of the time, Pallas kernels for 13%

profile of v5, /device:TPU:0, one launch (start us, length us, event | category | flops | bytes accessed | tf_op | source)
XLA Modules:
  0.0 174.9 jit_solution(17907186700083317160)
XLA Ops:
  7.2 0.7 add_bitcast_fusion
  7.9 0.7 and_reduce_fusion
  8.6 1.1 bitcast_select_fusion
  9.8 0.8 constant_dynamic-slice_fusion
  10.6 3.0 %collective-permute-start.1 = (bf16[64,2048]{1,0:T(8,128)(2,1)S(1)}, bf16[64,2048]{1,0:T(8,128)(2,1)S(1)}, u32[]{:S(2)}, u32[]{:S(2)}) collective-permute-start(bf16[64,2048]{1,0:T(8,128)(2,1)S(1)} %get-tuple-element.11), channel_id=1, source_target_pairs={{0,16},{16,0},{1,17},{17,1},{2,18},{18,2},{3,19},{19,3},{4,20},{20... | collective-permute-start | bytes 786440 | tf_op jit(solution)/shard_map/ppermute | solution.py:153
  13.7 4.6 %dynamic-slice_bitcast_fusion = bf16[2048,1024]{1,0:T(8,128)(2,1)} fusion(bf16[1,4096,1024]{2,1,0:T(8,128)(2,1)} %param.8, s32[]{:T(128)S(6)} %select_n.13), kind=kLoop, calls=%fused_computation | loop fusion | bytes 8388612 | tf_op jit(solution)/shard_map/dynamic_slice | solution.py:156
  20.5 0.7 copy-done.4
  21.9 0.7 fusion.11
  23.9 0.7 fusion.8
  25.9 0.7 fusion.5
  29.2 0.7 fusion
  29.9 6.3 %all-to-all-start = ((bf16[16,64,1024]{2,1,0:T(8,128)(2,1)}), bf16[16,64,1024]{2,1,0:T(8,128)(2,1)S(1)}, u32[]{:S(2)}, u32[]{:S(2)}) async-start(bf16[16,64,1024]{2,1,0:T(8,128)(2,1)} %fusion), calls=%async_computation | async-start | bytes 4194304 | tf_op jit(solution)/shard_map/all_to_all | solution.py:167
  36.3 1.5 collective-permute-start
  37.8 72.9 %collective-permute-done = s32[2]{0:T(128)S(1)} collective-permute-done((s32[2]{0:T(128)S(1)}, s32[2]{0:T(128)S(1)}, u32[]{:S(2)}, u32[]{:S(2)}) %collective-permute-start) | collective-permute-done | bytes 40 | tf_op jit(solution)/shard_map/ppermute | solution.py:153
  110.8 1.1 collective-permute-start.4
  111.9 1.1 fusion.16
  113.0 1.0 collective-permute-start.5
  114.0 1.0 collective-permute-start.3
  115.0 2.2 %copy-done.2 = bf16[1024,2048]{1,0:T(8,128)(2,1)S(1)} copy-done((bf16[1024,2048]{1,0:T(8,128)(2,1)S(1)}, bf16[1024,2048]{1,0:T(8,128)(2,1)}, u32[]{:S(2)}) %copy-start.2) | copy-done | bytes 4194328
  117.2 10.5 %shard_map.64.refs_0_ = bf16[2048,1024]{1,0:T(8,128)(2,1)S(1)} custom-call(s32[2,2]{1,0:T(2,128)S(1)} %pad_add_fusion.table_ref, bf16[16,1,64,2048]{3,2,1,0:T(8,128)(2,1)S(1)} %bitcast.85, bf16[1024,1024]{1,0:T(8,128)(2,1)S(1)} %bitcast.84), custom_call_target="tpu_custom_call" | custom-call | flops 8589934592 | bytes 4194304 | tf_op jit(solution)/shard_map/pallas_call | solution.py:52
  127.7 2.0 %copy-done = bf16[2048,1024]{1,0:T(8,128)(2,1)} copy-done((bf16[2048,1024]{1,0:T(8,128)(2,1)}, bf16[2048,1024]{1,0:T(8,128)(2,1)S(1)}, u32[]{:S(2)}) %copy-start) | copy-done | bytes 4194328
  129.7 18.6 %collective-permute-done.5.refs_3_ = bf16[1024,256]{1,0:T(8,128)(2,1)} collective-permute-done((bf16[1024,256]{1,0:T(8,128)(2,1)}, bf16[1024,256]{1,0:T(8,128)(2,1)}, u32[]{:S(2)}, u32[]{:S(2)}) %collective-permute-start.5) | collective-permute-done | bytes 524320 | tf_op jit(solution)/shard_map/ppermute | solution.py:153
  148.3 12.5 %shard_map.65.refs_5_ = bf16[2048,1024]{1,0:T(8,128)(2,1)} custom-call(s32[2,2]{1,0:T(2,128)} %copy-done.1, bf16[2048,1024]{1,0:T(8,128)(2,1)} %copy-done, bf16[16,1,64,2048]{3,2,1,0:T(8,128)(2,1)} %bitcast.88, bf16[1024,512]{1,0:T(8,128)(2,1)} %collective-permute-done.4.refs_2_, bf16[1024,256]{1,0:T(8,128)(2,1)} %collective-permute-done.5.refs_3_, ...), custom_call_target="tpu_custom_call" | custom-call | flops 6442450944 | bytes 15728640 | tf_op jit(solution)/shard_map/pallas_call | solution.py:113
  160.8 7.2 %shard_map.66 = bf16[2048,1024]{1,0:T(8,128)(2,1)} custom-call(s32[2,2]{1,0:T(2,128)} %copy-done.1, bf16[2048,1024]{1,0:T(8,128)(2,1)} %copy-done, bf16[16,1,64,2048]{3,2,1,0:T(8,128)(2,1)} %bitcast.89, bf16[1024,256]{1,0:T(8,128)(2,1)} %collective-permute-done.3.refs_2_, bf16[4096,1024]{1,0:T(8,128)(2,1)} %bitcast.87, ...), custom_call_target="tpu_custom_call", output_to_operand_aliasing={{}: (6, {})} | custom-call | flops 2147483648 | bytes 5242880 | tf_op jit(solution)/shard_map/pallas_call | solution.py:113
  (37 shorter events, 8.5 us)
Async XLA Ops:
  6.5 108.5 %all-gather.5.cloned.1.call-start = ((), (), s32[]{:S(2)}) async-start(), calls=%async_computation.1 | async-start | bytes 4456448 | tf_op jit(solution)/shard_map/all_gather | solution.py:163
  10.6 137.7 %all-gather.7.cloned.1.call-start = ((), (), s32[]{:S(2)}) async-start(), calls=%async_computation.2 | async-start | bytes 4456448 | tf_op jit(solution)/shard_map/all_gather | solution.py:163
  10.6 7.8 %copy-start.3 = (bf16[1,64,16384]{2,1,0:T(8,128)(2,1)S(1)}, bf16[1,64,16384]{2,1,0:T(8,128)(2,1)}, u32[]{:S(2)}) copy-start(bf16[1,64,16384]{2,1,0:T(8,128)(2,1)} %param.7) | copy-start | bytes 6291460
  10.6 9.8 %collective-permute-start.1 = (bf16[64,2048]{1,0:T(8,128)(2,1)S(1)}, bf16[64,2048]{1,0:T(8,128)(2,1)S(1)}, u32[]{:S(2)}, u32[]{:S(2)}) collective-permute-start(bf16[64,2048]{1,0:T(8,128)(2,1)S(1)} %get-tuple-element.11), channel_id=1, source_target_pairs={{0,16},{16,0},{1,17},{17,1},{2,18},{18,2},{3,19},{19,3},{4,20},{20... | collective-permute-start | bytes 786440 | tf_op jit(solution)/shard_map/ppermute | solution.py:153
  18.3 92.4 %collective-permute-start.2 = (bf16[2048,1024]{1,0:T(8,128)(2,1)}, bf16[2048,1024]{1,0:T(8,128)(2,1)}, u32[]{:S(2)}, u32[]{:S(2)}) collective-permute-start(bf16[2048,1024]{1,0:T(8,128)(2,1)} %dynamic-slice_bitcast_fusion), channel_id=1, source_target_pairs={{0,16},{16,0},{1,17},{17,1},{2,18},{18,2},{3,19},{19,3},{4,20},{20... | collective-permute-start | bytes 12582920 | tf_op jit(solution)/shard_map/ppermute | solution.py:153
  20.5 0.7 copy-start.4
  29.9 80.8 %all-to-all-start = ((bf16[16,64,1024]{2,1,0:T(8,128)(2,1)}), bf16[16,64,1024]{2,1,0:T(8,128)(2,1)S(1)}, u32[]{:S(2)}, u32[]{:S(2)}) async-start(bf16[16,64,1024]{2,1,0:T(8,128)(2,1)} %fusion), calls=%async_computation | async-start | bytes 4194304 | tf_op jit(solution)/shard_map/all_to_all | solution.py:167
  36.3 74.4 %collective-permute-start = (s32[2]{0:T(128)S(1)}, s32[2]{0:T(128)S(1)}, u32[]{:S(2)}, u32[]{:S(2)}) collective-permute-start(s32[2]{0:T(128)S(1)} %pad_add_fusion.1), channel_id=1, source_target_pairs={{0,16},{16,0},{1,17},{17,1},{2,18},{18,2},{3,19},{19,3},{4,20},{20... | collective-permute-start | bytes 32 | tf_op jit(solution)/shard_map/ppermute | solution.py:153
  110.7 4.3 %copy-start.1 = (s32[2,2]{1,0:T(2,128)}, s32[2,2]{1,0:T(2,128)S(1)}, u32[]{:S(2)}) copy-start(s32[2,2]{1,0:T(2,128)S(1)} %pad_add_fusion.table_ref) | copy-start | bytes 52
  110.8 37.5 %collective-permute-start.4 = (bf16[1024,512]{1,0:T(8,128)(2,1)S(1)}, bf16[1024,512]{1,0:T(8,128)(2,1)}, u32[]{:S(2)}, u32[]{:S(2)}) collective-permute-start(bf16[1024,512]{1,0:T(8,128)(2,1)S(1)} %slice.74), channel_id=1, source_target_pairs={{0,16},{16,0},{1,17},{17,1},{2,18},{18,2},{3,19},{19,3},{4,20},{20... | collective-permute-start | bytes 3145736 | tf_op jit(solution)/shard_map/ppermute | solution.py:153
  113.0 35.3 %collective-permute-start.5 = (bf16[1024,256]{1,0:T(8,128)(2,1)}, bf16[1024,256]{1,0:T(8,128)(2,1)}, u32[]{:S(2)}, u32[]{:S(2)}) collective-permute-start(bf16[1024,256]{1,0:T(8,128)(2,1)} %get-tuple-element.9), channel_id=1, source_target_pairs={{0,16},{16,0},{1,17},{17,1},{2,18},{18,2},{3,19},{19,3},{4,20},{20... | collective-permute-start | bytes 1572872 | tf_op jit(solution)/shard_map/ppermute | solution.py:153
  114.0 46.9 %collective-permute-start.3 = (bf16[1024,256]{1,0:T(8,128)(2,1)}, bf16[1024,256]{1,0:T(8,128)(2,1)}, u32[]{:S(2)}, u32[]{:S(2)}) collective-permute-start(bf16[1024,256]{1,0:T(8,128)(2,1)} %get-tuple-element.10), channel_id=1, source_target_pairs={{0,16},{16,0},{1,17},{17,1},{2,18},{18,2},{3,19},{19,3},{4,20},{20... | collective-permute-start | bytes 1572872 | tf_op jit(solution)/shard_map/ppermute | solution.py:153
  115.0 2.2 %copy-start.2 = (bf16[1024,2048]{1,0:T(8,128)(2,1)S(1)}, bf16[1024,2048]{1,0:T(8,128)(2,1)}, u32[]{:S(2)}) copy-start(bf16[1024,2048]{1,0:T(8,128)(2,1)} %all-gather.5.cloned.1.call-done) | copy-start | bytes 12582916
  127.7 2.0 %copy-start = (bf16[2048,1024]{1,0:T(8,128)(2,1)}, bf16[2048,1024]{1,0:T(8,128)(2,1)S(1)}, u32[]{:S(2)}) copy-start(bf16[2048,1024]{1,0:T(8,128)(2,1)S(1)} %shard_map.64.refs_0_) | copy-start | bytes 12582916
Sparse Core Ops, SparseCore 0:
  10.7 79.9 all-gather.4
  92.9 51.2 all-gather.6

commit v6 on v5

--- a/solution.py
+++ b/solution.py
@@ -96,7 +96,7 @@
     high, width = fisher.shape
     joined = len(g) // (tasks - 1)
     some = sum(part.shape[1] for part in g[:joined])
-    block = tile(high, 512 if joined > 1 else 1024)
+    block = tile(high, 1024)
     here = pl.BlockSpec((block, some), lambda i, s: (i, piece))
     own_spec = pl.BlockSpec((block, some), lambda i, s: (s[0, s.shape[1] - 1] * (high // block) + i, piece))
     x_specs = [

time: 175 us -> 177 us (1.011)
  transfers between devices with their start and end apart: 9 -> 9, of which waited for: 2 -> 2; matrix products, arithmetic and copies ran while one was open for 9% -> 9% of each run, Pallas kernels for 13% -> 14%
where the time goes in v6:
time: 177 us; the launch traced here: 176 us
  waiting for transfers between devices  91.5 us (52%)
  Pallas kernels  31.6 us (18%)
  local copies, waits for them, and re-layouts  22.1 us (12%)
  between operations  14.2 us (8%)
  starting transfers between devices  14.1 us (8%)
  other arithmetic  2.74 us (2%)
    ppermute x6, waiting for transfers between devices, hand_on(): lax.ppermute(value, 'task', [(i, (i + step) % tasks) for i in range(tasks)])  91.5 us
    pallas_call x2, Pallas kernels, merge_columns(): pl.pallas_call(functools.partial(merge_kernel, tasks, slots, min((tile(pa...  21.1 us
    unnamed x25, local copies, waits for them, and re-layouts  14.8 us
    pallas_call x1, Pallas kernels, fisher_of(): pl.pallas_call(functools.partial(fisher_kernel, task, slots, tile(width,...  10.5 us
    ppermute x6, starting transfers between devices, hand_on(): lax.ppermute(value, 'task', [(i, (i + step) % tasks) for i in range(tasks)])  7.79 us
    all_to_all x1, starting transfers between devices, per_device(): lax.all_to_all(blocks, 'shard', split_axis=0, concat_axis=0, tiled=True)  6.32 us
    dynamic_slice x2, local copies, waits for them, and re-layouts, block_of(): lax.dynamic_slice_in_dim(value, lax.rem(mine + step, tasks) * high, high,...  5.41 us
  transfers between devices with their start and end apart: 9, of which 2 were waited for; matrix products, arithmetic and copies ran while one was open for 9% of the time, Pallas kernels for 14%

profile of v6, /device:TPU:0, one launch (start us, length us, event | category | flops | bytes accessed | tf_op | source)
XLA Modules:
  0.0 176.3 jit_solution(5604559078864389623)
XLA Ops:
  7.2 0.7 add_bitcast_fusion
  7.9 0.7 and_reduce_fusion
  8.6 1.1 bitcast_select_fusion
  9.8 0.8 constant_dynamic-slice_fusion
  10.6 3.0 %collective-permute-start.1 = (bf16[64,2048]{1,0:T(8,128)(2,1)S(1)}, bf16[64,2048]{1,0:T(8,128)(2,1)S(1)}, u32[]{:S(2)}, u32[]{:S(2)}) collective-permute-start(bf16[64,2048]{1,0:T(8,128)(2,1)S(1)} %get-tuple-element.11), channel_id=1, source_target_pairs={{0,16},{16,0},{1,17},{17,1},{2,18},{18,2},{3,19},{19,3},{4,20},{20... | collective-permute-start | bytes 786440 | tf_op jit(solution)/shard_map/ppermute | solution.py:153
  13.7 4.6 %dynamic-slice_bitcast_fusion = bf16[2048,1024]{1,0:T(8,128)(2,1)} fusion(bf16[1,4096,1024]{2,1,0:T(8,128)(2,1)} %param.8, s32[]{:T(128)S(6)} %select_n.13), kind=kLoop, calls=%fused_computation | loop fusion | bytes 8388612 | tf_op jit(solution)/shard_map/dynamic_slice | solution.py:156
  20.5 0.7 copy-done.4
  21.9 0.7 fusion.11
  23.9 0.7 fusion.8
  25.9 0.7 fusion.5
  29.2 0.7 fusion
  29.9 6.3 %all-to-all-start = ((bf16[16,64,1024]{2,1,0:T(8,128)(2,1)}), bf16[16,64,1024]{2,1,0:T(8,128)(2,1)S(1)}, u32[]{:S(2)}, u32[]{:S(2)}) async-start(bf16[16,64,1024]{2,1,0:T(8,128)(2,1)} %fusion), calls=%async_computation | async-start | bytes 4194304 | tf_op jit(solution)/shard_map/all_to_all | solution.py:167
  36.3 1.5 collective-permute-start
  37.8 72.9 %collective-permute-done = s32[2]{0:T(128)S(1)} collective-permute-done((s32[2]{0:T(128)S(1)}, s32[2]{0:T(128)S(1)}, u32[]{:S(2)}, u32[]{:S(2)}) %collective-permute-start) | collective-permute-done | bytes 40 | tf_op jit(solution)/shard_map/ppermute | solution.py:153
  110.8 1.1 collective-permute-start.4
  111.9 1.1 fusion.16
  113.0 1.0 collective-permute-start.5
  114.0 1.0 collective-permute-start.3
  115.0 2.2 %copy-done.2 = bf16[1024,2048]{1,0:T(8,128)(2,1)S(1)} copy-done((bf16[1024,2048]{1,0:T(8,128)(2,1)S(1)}, bf16[1024,2048]{1,0:T(8,128)(2,1)}, u32[]{:S(2)}) %copy-start.2) | copy-done | bytes 4194328
  117.2 10.5 %shard_map.64.refs_0_ = bf16[2048,1024]{1,0:T(8,128)(2,1)S(1)} custom-call(s32[2,2]{1,0:T(2,128)S(1)} %pad_add_fusion.table_ref, bf16[16,1,64,2048]{3,2,1,0:T(8,128)(2,1)S(1)} %bitcast.85, bf16[1024,1024]{1,0:T(8,128)(2,1)S(1)} %bitcast.84), custom_call_target="tpu_custom_call" | custom-call | flops 8589934592 | bytes 4194304 | tf_op jit(solution)/shard_map/pallas_call | solution.py:52
  127.7 2.0 %copy-done = bf16[2048,1024]{1,0:T(8,128)(2,1)} copy-done((bf16[2048,1024]{1,0:T(8,128)(2,1)}, bf16[2048,1024]{1,0:T(8,128)(2,1)S(1)}, u32[]{:S(2)}) %copy-start) | copy-done | bytes 4194328
  129.7 18.6 %collective-permute-done.5.refs_3_ = bf16[1024,256]{1,0:T(8,128)(2,1)} collective-permute-done((bf16[1024,256]{1,0:T(8,128)(2,1)}, bf16[1024,256]{1,0:T(8,128)(2,1)}, u32[]{:S(2)}, u32[]{:S(2)}) %collective-permute-start.5) | collective-permute-done | bytes 524320 | tf_op jit(solution)/shard_map/ppermute | solution.py:153
  148.3 13.9 %shard_map.65.refs_5_ = bf16[2048,1024]{1,0:T(8,128)(2,1)} custom-call(s32[2,2]{1,0:T(2,128)} %copy-done.1, bf16[2048,1024]{1,0:T(8,128)(2,1)} %copy-done, bf16[16,1,64,2048]{3,2,1,0:T(8,128)(2,1)} %bitcast.88, bf16[1024,512]{1,0:T(8,128)(2,1)} %collective-permute-done.4.refs_2_, bf16[1024,256]{1,0:T(8,128)(2,1)} %collective-permute-done.5.refs_3_, ...), custom_call_target="tpu_custom_call" | custom-call | flops 6442450944 | bytes 15728640 | tf_op jit(solution)/shard_map/pallas_call | solution.py:113
  162.2 7.2 %shard_map.66 = bf16[2048,1024]{1,0:T(8,128)(2,1)} custom-call(s32[2,2]{1,0:T(2,128)} %copy-done.1, bf16[2048,1024]{1,0:T(8,128)(2,1)} %copy-done, bf16[16,1,64,2048]{3,2,1,0:T(8,128)(2,1)} %bitcast.89, bf16[1024,256]{1,0:T(8,128)(2,1)} %collective-permute-done.3.refs_2_, bf16[4096,1024]{1,0:T(8,128)(2,1)} %bitcast.87, ...), custom_call_target="tpu_custom_call", output_to_operand_aliasing={{}: (6, {})} | custom-call | flops 2147483648 | bytes 5242880 | tf_op jit(solution)/shard_map/pallas_call | solution.py:113
  (37 shorter events, 8.5 us)
Async XLA Ops:
  6.5 108.5 %all-gather.5.cloned.1.call-start = ((), (), s32[]{:S(2)}) async-start(), calls=%async_computation.1 | async-start | bytes 4456448 | tf_op jit(solution)/shard_map/all_gather | solution.py:163
  10.6 137.7 %all-gather.7.cloned.1.call-start = ((), (), s32[]{:S(2)}) async-start(), calls=%async_computation.2 | async-start | bytes 4456448 | tf_op jit(solution)/shard_map/all_gather | solution.py:163
  10.6 7.8 %copy-start.3 = (bf16[1,64,16384]{2,1,0:T(8,128)(2,1)S(1)}, bf16[1,64,16384]{2,1,0:T(8,128)(2,1)}, u32[]{:S(2)}) copy-start(bf16[1,64,16384]{2,1,0:T(8,128)(2,1)} %param.7) | copy-start | bytes 6291460
  10.6 9.8 %collective-permute-start.1 = (bf16[64,2048]{1,0:T(8,128)(2,1)S(1)}, bf16[64,2048]{1,0:T(8,128)(2,1)S(1)}, u32[]{:S(2)}, u32[]{:S(2)}) collective-permute-start(bf16[64,2048]{1,0:T(8,128)(2,1)S(1)} %get-tuple-element.11), channel_id=1, source_target_pairs={{0,16},{16,0},{1,17},{17,1},{2,18},{18,2},{3,19},{19,3},{4,20},{20... | collective-permute-start | bytes 786440 | tf_op jit(solution)/shard_map/ppermute | solution.py:153
  18.3 92.4 %collective-permute-start.2 = (bf16[2048,1024]{1,0:T(8,128)(2,1)}, bf16[2048,1024]{1,0:T(8,128)(2,1)}, u32[]{:S(2)}, u32[]{:S(2)}) collective-permute-start(bf16[2048,1024]{1,0:T(8,128)(2,1)} %dynamic-slice_bitcast_fusion), channel_id=1, source_target_pairs={{0,16},{16,0},{1,17},{17,1},{2,18},{18,2},{3,19},{19,3},{4,20},{20... | collective-permute-start | bytes 12582920 | tf_op jit(solution)/shard_map/ppermute | solution.py:153
  20.5 0.7 copy-start.4
  29.9 80.8 %all-to-all-start = ((bf16[16,64,1024]{2,1,0:T(8,128)(2,1)}), bf16[16,64,1024]{2,1,0:T(8,128)(2,1)S(1)}, u32[]{:S(2)}, u32[]{:S(2)}) async-start(bf16[16,64,1024]{2,1,0:T(8,128)(2,1)} %fusion), calls=%async_computation | async-start | bytes 4194304 | tf_op jit(solution)/shard_map/all_to_all | solution.py:167
  36.3 74.4 %collective-permute-start = (s32[2]{0:T(128)S(1)}, s32[2]{0:T(128)S(1)}, u32[]{:S(2)}, u32[]{:S(2)}) collective-permute-start(s32[2]{0:T(128)S(1)} %pad_add_fusion.1), channel_id=1, source_target_pairs={{0,16},{16,0},{1,17},{17,1},{2,18},{18,2},{3,19},{19,3},{4,20},{20... | collective-permute-start | bytes 32 | tf_op jit(solution)/shard_map/ppermute | solution.py:153
  110.7 4.3 %copy-start.1 = (s32[2,2]{1,0:T(2,128)}, s32[2,2]{1,0:T(2,128)S(1)}, u32[]{:S(2)}) copy-start(s32[2,2]{1,0:T(2,128)S(1)} %pad_add_fusion.table_ref) | copy-start | bytes 52
  110.8 37.5 %collective-permute-start.4 = (bf16[1024,512]{1,0:T(8,128)(2,1)S(1)}, bf16[1024,512]{1,0:T(8,128)(2,1)}, u32[]{:S(2)}, u32[]{:S(2)}) collective-permute-start(bf16[1024,512]{1,0:T(8,128)(2,1)S(1)} %slice.74), channel_id=1, source_target_pairs={{0,16},{16,0},{1,17},{17,1},{2,18},{18,2},{3,19},{19,3},{4,20},{20... | collective-permute-start | bytes 3145736 | tf_op jit(solution)/shard_map/ppermute | solution.py:153
  113.0 35.3 %collective-permute-start.5 = (bf16[1024,256]{1,0:T(8,128)(2,1)}, bf16[1024,256]{1,0:T(8,128)(2,1)}, u32[]{:S(2)}, u32[]{:S(2)}) collective-permute-start(bf16[1024,256]{1,0:T(8,128)(2,1)} %get-tuple-element.9), channel_id=1, source_target_pairs={{0,16},{16,0},{1,17},{17,1},{2,18},{18,2},{3,19},{19,3},{4,20},{20... | collective-permute-start | bytes 1572872 | tf_op jit(solution)/shard_map/ppermute | solution.py:153
  114.0 48.2 %collective-permute-start.3 = (bf16[1024,256]{1,0:T(8,128)(2,1)}, bf16[1024,256]{1,0:T(8,128)(2,1)}, u32[]{:S(2)}, u32[]{:S(2)}) collective-permute-start(bf16[1024,256]{1,0:T(8,128)(2,1)} %get-tuple-element.10), channel_id=1, source_target_pairs={{0,16},{16,0},{1,17},{17,1},{2,18},{18,2},{3,19},{19,3},{4,20},{20... | collective-permute-start | bytes 1572872 | tf_op jit(solution)/shard_map/ppermute | solution.py:153
  115.0 2.2 %copy-start.2 = (bf16[1024,2048]{1,0:T(8,128)(2,1)S(1)}, bf16[1024,2048]{1,0:T(8,128)(2,1)}, u32[]{:S(2)}) copy-start(bf16[1024,2048]{1,0:T(8,128)(2,1)} %all-gather.5.cloned.1.call-done) | copy-start | bytes 12582916
  127.7 2.0 %copy-start = (bf16[2048,1024]{1,0:T(8,128)(2,1)}, bf16[2048,1024]{1,0:T(8,128)(2,1)S(1)}, u32[]{:S(2)}) copy-start(bf16[2048,1024]{1,0:T(8,128)(2,1)S(1)} %shard_map.64.refs_0_) | copy-start | bytes 12582916
Sparse Core Ops, SparseCore 0:
  10.7 79.9 all-gather.4
  92.9 51.2 all-gather.6
